TPU v7x, 256 devices: a whole 4x4x8 slice. The times are simulated.
256 devices in a mesh: ctx: 16 (over y_lo, x, core), head: 16 (over y_hi, z).
Axes of the slice: x: 4, y: 4 (y_hi: 2, y_lo: 2; y = y_hi * 2 + y_lo), z: 8, core: 2. Of those that a mesh axis runs over, the one named last changes fastest.
Arguments:
- layer_input: bfloat16 [5120, 5120], P('ctx', 'head'), may hold values from -0.29882812 to 0.29882812
- query_heads: bfloat16 [5120, 4096], P('ctx', 'head'), may hold values from -8 to 8
- key_heads: bfloat16 [5120, 4096], P('ctx', 'head'), may hold values from -8 to 8
- value_heads: bfloat16 [5120, 4096], P('ctx', 'head'), may hold values from -6 to 6
- map_one_out: bfloat16 [5120, 4096], P('ctx', 'head'), may hold values from -3 to 3
- map_two_out: bfloat16 [5120, 4096], P('ctx', 'head'), may hold values from -3 to 3
- grad_out: bfloat16 [5120, 4096], P('ctx', 'head'), may hold values from -6 to 6
- saved_lse: float32 [2, 16, 5120], P(None, 'head', 'ctx'), as said below
- lambdas: float32 [16], P('head'), may hold values from 0.2 to 0.8
- block_order: int32 [16], replicated, may hold values from 0 to 15, as said below
Outputs:
- grad_query: bfloat16 [5120, 4096], P('ctx', 'head')
- grad_key: bfloat16 [5120, 4096], P('ctx', 'head')
- grad_value: bfloat16 [5120, 4096], P('ctx', 'head')
- weight_grad: float32 [3, 5120, 4096], P(None, 'ctx', 'head')
Inputs may be any that keep to these rules, and one draw needn't show every extreme that they name: `block_order`: a permutation of 0 to 15. saved_lse[m, h, r] is the natural logarithm of the sum, over the keys visible to token r, of exp of the map m scores of head h, q_m k_m^T / sqrt(128).
All inputs are finite; a program needn't handle non-finite values.
Results may differ from a plain program's by a relative error of at most 0.005.
Values may be sent and summed in bfloat16 or wider, within the bound.
A program may use at most 64 MiB of HBM per device.

v0:
```python
import jax
import jax.numpy as jnp
from jax import lax
from jax.sharding import PartitionSpec as P

HALF = 128


score_scale = 0.08838834764831845


def from_behind(shard, axis, by):
    devices = lax.axis_size(axis)
    return lax.ppermute(shard, axis, [(i, (i + by) % devices) for i in range(devices)])


def block_grads(query_side, key_side, query_block, key_block, lambdas):
    queries, grad_rows, row_stats = query_side
    key_rows, values = key_side
    length = queries.shape[0]
    offsets = jnp.arange(length, dtype=jnp.int32)
    visible = (key_block * length + offsets)[None, :] <= (query_block * length + offsets)[:, None]
    score_one = (
        jnp.einsum(
            "qhd,khd->hqk",
            queries[..., :HALF],
            key_rows[..., :HALF],
            preferred_element_type=jnp.float32,
        )
        * score_scale
    )
    score_two = (
        jnp.einsum(
            "qhd,khd->hqk",
            queries[..., HALF:],
            key_rows[..., HALF:],
            preferred_element_type=jnp.float32,
        )
        * score_scale
    )
    probs_one = jnp.exp(jnp.where(visible[None], score_one - row_stats[0][:, :, None], -1e30))
    probs_two = jnp.exp(jnp.where(visible[None], score_two - row_stats[1][:, :, None], -1e30))
    upstream = jnp.einsum("qhd,khd->hqk", grad_rows, values, preferred_element_type=jnp.float32)
    weight = lambdas[:, None, None]
    slope_one = (probs_one * (upstream - row_stats[2][:, :, None])).astype(jnp.bfloat16)
    slope_two = (probs_two * (-weight * upstream - row_stats[3][:, :, None])).astype(jnp.bfloat16)
    mixture = (probs_one - weight * probs_two).astype(jnp.bfloat16)
    query_part = (
        jnp.concatenate(
            [
                jnp.einsum(
                    "hqk,khd->qhd",
                    slope_one,
                    key_rows[..., :HALF],
                    preferred_element_type=jnp.float32,
                ),
                jnp.einsum(
                    "hqk,khd->qhd",
                    slope_two,
                    key_rows[..., HALF:],
                    preferred_element_type=jnp.float32,
                ),
            ],
            axis=2,
        )
        * score_scale
    )
    key_part = (
        jnp.concatenate(
            [
                jnp.einsum(
                    "hqk,qhd->khd",
                    slope_one,
                    queries[..., :HALF],
                    preferred_element_type=jnp.float32,
                ),
                jnp.einsum(
                    "hqk,qhd->khd",
                    slope_two,
                    queries[..., HALF:],
                    preferred_element_type=jnp.float32,
                ),
            ],
            axis=2,
        )
        * score_scale
    )
    value_part = jnp.einsum("hqk,qhd->khd", mixture, grad_rows, preferred_element_type=jnp.float32)
    return (query_part, key_part, value_part)


def move_pair(light_part, heavy_part, direction):
    light_one, light_two = light_part
    heavy_one, heavy_two = heavy_part
    light_part = from_behind((light_one, light_two), "ctx", direction)
    heavy_part = from_behind((heavy_one, heavy_two), "ctx", direction)
    return (light_part, heavy_part)


def send_home(heavy_part, direction, steps, cycle_size):
    distance = -direction * steps % cycle_size
    heavy_one, heavy_two = heavy_part
    return from_behind((heavy_one, heavy_two), "ctx", distance)


def travel(light_part, heavy_part, local_part, visitor):
    cycle_size = lax.axis_size("ctx")
    device_slot = lax.axis_index("ctx")

    def advance(light_now, heavy_now, local_now, step_index, direction):
        light_now, heavy_now = move_pair(light_now, heavy_now, direction)
        source = (device_slot - direction * (step_index + 1)) % cycle_size
        heavy_now, local_now = visitor(light_now, heavy_now, source, local_now)
        return (light_now, heavy_now, local_now)

    def single(step_index, loop_state):
        return advance(loop_state[0], loop_state[1], loop_state[2], step_index, 1)

    light_end, heavy_end, local_end = lax.fori_loop(
        0, cycle_size - 1, single, (light_part, heavy_part, local_part)
    )
    return (send_home(heavy_end, 1, cycle_size - 1, cycle_size), local_end)


def body(
    layer_input,
    query_heads,
    key_heads,
    value_heads,
    map_one_out,
    map_two_out,
    grad_out,
    saved_lse,
    lambdas,
    block_order,
):
    length = query_heads.shape[0]
    head_count = query_heads.shape[1] // (2 * HALF)
    queries = query_heads.reshape(length, head_count, 2 * HALF)
    key_rows = key_heads.reshape(length, head_count, 2 * HALF)
    values = value_heads.reshape(length, head_count, 2 * HALF)
    grad_rows = grad_out.reshape(length, head_count, 2 * HALF)
    out_one = map_one_out.reshape(length, head_count, 2 * HALF)
    out_two = map_two_out.reshape(length, head_count, 2 * HALF)
    device_slot = lax.axis_index("ctx")
    own_block = block_order[device_slot]
    inner_one = jnp.sum(grad_rows.astype(jnp.float32) * out_one.astype(jnp.float32), axis=2).T
    inner_two = (
        -lambdas[:, None]
        * jnp.sum(grad_rows.astype(jnp.float32) * out_two.astype(jnp.float32), axis=2).T
    )
    row_stats = jnp.concatenate([saved_lse, jnp.stack([inner_one, inner_two])], axis=0)
    own_query = (queries, grad_rows, row_stats)
    own_keys = (key_rows, values)
    query_acc, key_acc, value_acc = block_grads(own_query, own_keys, own_block, own_block, lambdas)
    blank_grad = jnp.zeros_like(query_acc)

    def visit_keys(light_now, heavy_now, source, local_now):
        pieces = block_grads(own_query, light_now, own_block, block_order[source], lambdas)
        return ((heavy_now[0] + pieces[1], heavy_now[1] + pieces[2]), local_now + pieces[0])

    returned, local_end = travel(
        (key_rows, values), (blank_grad, blank_grad), blank_grad, visit_keys
    )
    query_acc = query_acc + local_end
    key_acc = key_acc + returned[0]
    value_acc = value_acc + returned[1]
    grad_query = query_acc.astype(jnp.bfloat16).reshape(length, head_count * 2 * HALF)
    grad_key = key_acc.astype(jnp.bfloat16).reshape(length, head_count * 2 * HALF)
    grad_value = value_acc.astype(jnp.bfloat16).reshape(length, head_count * 2 * HALF)
    full_rows = lax.all_gather(layer_input, "head", axis=1, tiled=True)
    columns = lax.all_to_all(full_rows, "ctx", split_axis=1, concat_axis=0, tiled=True)
    contract_dims = (((0,), (0,)), ((), ()))
    pieces = (
        lax.all_gather(grad_query, "ctx", axis=0, tiled=True),
        lax.all_gather(grad_key, "ctx", axis=0, tiled=True),
        lax.all_gather(grad_value, "ctx", axis=0, tiled=True),
    )
    totals = (
        lax.dot_general(columns, pieces[0], contract_dims, preferred_element_type=jnp.float32),
        lax.dot_general(columns, pieces[1], contract_dims, preferred_element_type=jnp.float32),
        lax.dot_general(columns, pieces[2], contract_dims, preferred_element_type=jnp.float32),
    )
    weight_grad = jnp.stack(totals)
    return (grad_query, grad_key, grad_value, weight_grad)


def solution(mesh):
    in_specs = (
        P("ctx", "head"),
        P("ctx", "head"),
        P("ctx", "head"),
        P("ctx", "head"),
        P("ctx", "head"),
        P("ctx", "head"),
        P("ctx", "head"),
        P(None, "head", "ctx"),
        P("head"),
        P(),
    )
    out_specs = (P("ctx", "head"), P("ctx", "head"), P("ctx", "head"), P(None, "ctx", "head"))
    return jax.shard_map(body, mesh=mesh, in_specs=in_specs, out_specs=out_specs, check_vma=False)
```

profile of v0, /device:TPU:8, one launch (start us, length us, event | category | flops | bytes accessed | tf_op | source)
XLA Modules:
  0.0 436.1 jit_solution(14891858826562807730)
XLA Ops:
  7.2 1.8 copy.15
  9.8 1.3 fusion.46
  12.9 1.2 dynamic_slice.13
  14.8 251.8 %while.24 = (s32[]{:T(128)}, bf16[320,1,256]{2,0,1:T(8,128)(2,1)S(1)}, bf16[320,1,256]{2,0,1:T(8,128)(2,1)S(1)}, f32[320,1,256]{2,0,1:T(8,128)S(1)}, f32[320,1,2...) while((s32[]{:T(128)}, ...), condition=%wide.region_3.4_spmd.clone, body=%wide.region_2.3_spmd.clone.sunk | while | flops 264807056 | bytes 15511156 | solution.py:119
  14.9 1.6 collective-permute-start
  16.7 1.6 collective-permute-start.3
  18.3 1.3 dynamic_slice.16
  21.0 2.5 collective-permute-done
  27.4 3.3 collective-permute-done.3
  33.0 1.3 dynamic_slice.16
  35.7 4.7 %collective-permute-done = bf16[320,1,256]{2,0,1:T(8,128)(2,1)S(1)} collective-permute-done((bf16[320,1,256]{2,0,1:T(8,128)(2,1)S(1)}, bf16[320,1,256]{2,0,1:T(8,128)(2,1)S(1)}, u32[]{:S(2)}, u32[]{:S(2)}) %collective-permute-start) | collective-permute-done | bytes 163872 | tf_op jit(solution)/shard_map/while/body/eval_jaxpr/ppermute | solution.py:14
  44.2 3.2 collective-permute-done.3
  48.9 1.3 dynamic_slice.16
  51.6 5.5 %collective-permute-done = bf16[320,1,256]{2,0,1:T(8,128)(2,1)S(1)} collective-permute-done((bf16[320,1,256]{2,0,1:T(8,128)(2,1)S(1)}, bf16[320,1,256]{2,0,1:T(8,128)(2,1)S(1)}, u32[]{:S(2)}, u32[]{:S(2)}) %collective-permute-start) | collective-permute-done | bytes 163872 | tf_op jit(solution)/shard_map/while/body/eval_jaxpr/ppermute | solution.py:14
  61.0 3.2 collective-permute-done.3
  65.7 1.3 dynamic_slice.16
  68.4 5.6 %collective-permute-done = bf16[320,1,256]{2,0,1:T(8,128)(2,1)S(1)} collective-permute-done((bf16[320,1,256]{2,0,1:T(8,128)(2,1)S(1)}, bf16[320,1,256]{2,0,1:T(8,128)(2,1)S(1)}, u32[]{:S(2)}, u32[]{:S(2)}) %collective-permute-start) | collective-permute-done | bytes 163872 | tf_op jit(solution)/shard_map/while/body/eval_jaxpr/ppermute | solution.py:14
  77.8 3.2 collective-permute-done.3
  82.5 1.3 dynamic_slice.16
  85.2 5.6 %collective-permute-done = bf16[320,1,256]{2,0,1:T(8,128)(2,1)S(1)} collective-permute-done((bf16[320,1,256]{2,0,1:T(8,128)(2,1)S(1)}, bf16[320,1,256]{2,0,1:T(8,128)(2,1)S(1)}, u32[]{:S(2)}, u32[]{:S(2)}) %collective-permute-start) | collective-permute-done | bytes 163872 | tf_op jit(solution)/shard_map/while/body/eval_jaxpr/ppermute | solution.py:14
  94.7 3.2 collective-permute-done.3
  99.4 1.3 dynamic_slice.16
  102.1 5.6 %collective-permute-done = bf16[320,1,256]{2,0,1:T(8,128)(2,1)S(1)} collective-permute-done((bf16[320,1,256]{2,0,1:T(8,128)(2,1)S(1)}, bf16[320,1,256]{2,0,1:T(8,128)(2,1)S(1)}, u32[]{:S(2)}, u32[]{:S(2)}) %collective-permute-start) | collective-permute-done | bytes 163872 | tf_op jit(solution)/shard_map/while/body/eval_jaxpr/ppermute | solution.py:14
  111.5 3.2 collective-permute-done.3
  116.3 1.3 dynamic_slice.16
  118.9 5.5 %collective-permute-done = bf16[320,1,256]{2,0,1:T(8,128)(2,1)S(1)} collective-permute-done((bf16[320,1,256]{2,0,1:T(8,128)(2,1)S(1)}, bf16[320,1,256]{2,0,1:T(8,128)(2,1)S(1)}, u32[]{:S(2)}, u32[]{:S(2)}) %collective-permute-start) | collective-permute-done | bytes 163872 | tf_op jit(solution)/shard_map/while/body/eval_jaxpr/ppermute | solution.py:14
  128.3 3.2 collective-permute-done.3
  133.0 1.3 dynamic_slice.16
  135.7 5.5 %collective-permute-done = bf16[320,1,256]{2,0,1:T(8,128)(2,1)S(1)} collective-permute-done((bf16[320,1,256]{2,0,1:T(8,128)(2,1)S(1)}, bf16[320,1,256]{2,0,1:T(8,128)(2,1)S(1)}, u32[]{:S(2)}, u32[]{:S(2)}) %collective-permute-start) | collective-permute-done | bytes 163872 | tf_op jit(solution)/shard_map/while/body/eval_jaxpr/ppermute | solution.py:14
  145.1 3.2 collective-permute-done.3
  149.8 1.3 dynamic_slice.16
  152.5 5.5 %collective-permute-done = bf16[320,1,256]{2,0,1:T(8,128)(2,1)S(1)} collective-permute-done((bf16[320,1,256]{2,0,1:T(8,128)(2,1)S(1)}, bf16[320,1,256]{2,0,1:T(8,128)(2,1)S(1)}, u32[]{:S(2)}, u32[]{:S(2)}) %collective-permute-start) | collective-permute-done | bytes 163872 | tf_op jit(solution)/shard_map/while/body/eval_jaxpr/ppermute | solution.py:14
  161.8 3.2 collective-permute-done.3
  166.5 1.3 dynamic_slice.16
  169.2 5.5 %collective-permute-done = bf16[320,1,256]{2,0,1:T(8,128)(2,1)S(1)} collective-permute-done((bf16[320,1,256]{2,0,1:T(8,128)(2,1)S(1)}, bf16[320,1,256]{2,0,1:T(8,128)(2,1)S(1)}, u32[]{:S(2)}, u32[]{:S(2)}) %collective-permute-start) | collective-permute-done | bytes 163872 | tf_op jit(solution)/shard_map/while/body/eval_jaxpr/ppermute | solution.py:14
  178.6 3.2 collective-permute-done.3
  183.3 1.3 dynamic_slice.16
  186.0 5.5 %collective-permute-done = bf16[320,1,256]{2,0,1:T(8,128)(2,1)S(1)} collective-permute-done((bf16[320,1,256]{2,0,1:T(8,128)(2,1)S(1)}, bf16[320,1,256]{2,0,1:T(8,128)(2,1)S(1)}, u32[]{:S(2)}, u32[]{:S(2)}) %collective-permute-start) | collective-permute-done | bytes 163872 | tf_op jit(solution)/shard_map/while/body/eval_jaxpr/ppermute | solution.py:14
  195.3 3.2 collective-permute-done.3
  200.0 1.3 dynamic_slice.16
  202.7 5.5 %collective-permute-done = bf16[320,1,256]{2,0,1:T(8,128)(2,1)S(1)} collective-permute-done((bf16[320,1,256]{2,0,1:T(8,128)(2,1)S(1)}, bf16[320,1,256]{2,0,1:T(8,128)(2,1)S(1)}, u32[]{:S(2)}, u32[]{:S(2)}) %collective-permute-start) | collective-permute-done | bytes 163872 | tf_op jit(solution)/shard_map/while/body/eval_jaxpr/ppermute | solution.py:14
  212.1 3.2 collective-permute-done.3
  216.8 1.3 dynamic_slice.16
  219.5 5.5 %collective-permute-done = bf16[320,1,256]{2,0,1:T(8,128)(2,1)S(1)} collective-permute-done((bf16[320,1,256]{2,0,1:T(8,128)(2,1)S(1)}, bf16[320,1,256]{2,0,1:T(8,128)(2,1)S(1)}, u32[]{:S(2)}, u32[]{:S(2)}) %collective-permute-start) | collective-permute-done | bytes 163872 | tf_op jit(solution)/shard_map/while/body/eval_jaxpr/ppermute | solution.py:14
  228.9 3.2 collective-permute-done.3
  233.6 1.3 dynamic_slice.16
  236.3 5.5 %collective-permute-done = bf16[320,1,256]{2,0,1:T(8,128)(2,1)S(1)} collective-permute-done((bf16[320,1,256]{2,0,1:T(8,128)(2,1)S(1)}, bf16[320,1,256]{2,0,1:T(8,128)(2,1)S(1)}, u32[]{:S(2)}, u32[]{:S(2)}) %collective-permute-start) | collective-permute-done | bytes 163872 | tf_op jit(solution)/shard_map/while/body/eval_jaxpr/ppermute | solution.py:14
  245.6 3.2 collective-permute-done.3
  250.3 1.3 dynamic_slice.16
  253.0 5.5 %collective-permute-done = bf16[320,1,256]{2,0,1:T(8,128)(2,1)S(1)} collective-permute-done((bf16[320,1,256]{2,0,1:T(8,128)(2,1)S(1)}, bf16[320,1,256]{2,0,1:T(8,128)(2,1)S(1)}, u32[]{:S(2)}, u32[]{:S(2)}) %collective-permute-start) | collective-permute-done | bytes 163872 | tf_op jit(solution)/shard_map/while/body/eval_jaxpr/ppermute | solution.py:14
  262.4 3.2 collective-permute-done.3
  267.4 1.2 fusion.52
  268.6 1.2 fusion.33
  269.9 1.3 multiply_convert_fusion.3
  271.1 4.2 collective-permute-done.5
  278.2 8.0 %collective-permute-done.4 = f32[320,1,256]{2,0,1:T(8,128)S(1)} collective-permute-done((f32[320,1,256]{2,0,1:T(8,128)S(1)}, f32[320,1,256]{2,0,1:T(8,128)S(1)}, u32[]{:S(2)}, u32[]{:S(2)}) %collective-permute-start.4) | collective-permute-done | bytes 327712 | tf_op jit(solution)/shard_map/ppermute | solution.py:14
  287.0 60.3 %all_to_all.19 = bf16[320,16,320]{0,2,1:T(8,128)(2,1)S(1)} all-to-all(bf16[320,16,320]{0,2,1:T(8,128)(2,1)} %bitcast.195), channel_id=1, replica_groups=mesh['ctx'=16,'head'=16] {'ctx'}, dimensions={1} | all-to-all | bytes 6553600 | tf_op jit(solution)/shard_map/all_to_all | solution.py:172
  347.3 4.2 copy.16
  351.5 7.3 %all_to_all.17 = bf16[5120,320]{0,1:T(8,128)(2,1)} reshape(bf16[16,320,320]{1,0,2:T(8,128)(2,1)} %copy.16) | data formatting | bytes 6553600 | tf_op jit(solution)/shard_map/all_to_all | solution.py:172
  358.9 3.8 fusion.40
  362.7 22.3 %all-gather.10.cloned.1.call-done = bf16[5120,1,256]{2,0,1:T(8,128)(2,1)} async-done(((bf16[320,1,256]{2,0,1:T(8,128)(2,1)}), bf16[5120,1,256]{2,0,1:T(8,128)(2,1)}) %all-gather.10.cloned.1.call-update) | async-done | bytes 2621456 | tf_op jit(solution)/shard_map/all_gather | solution.py:175
  385.0 3.7 fusion.34
  388.8 36.0 %all-gather.12.cloned.1.call-done = bf16[5120,1,256]{2,0,1:T(8,128)(2,1)} async-done(((bf16[320,1,256]{2,0,1:T(8,128)(2,1)}), bf16[5120,1,256]{2,0,1:T(8,128)(2,1)}) %all-gather.12.cloned.1.call-update) | async-done | bytes 2621456 | tf_op jit(solution)/shard_map/all_gather | solution.py:176
  424.8 3.7 fusion.37
  (471 shorter events, 96.5 us)
Async XLA Ops:
  7.2 279.8 %all-gather.8.cloned.1.call-start = ((), (), s32[]{:S(2)}) async-start(), calls=%async_computation.1 | async-start | bytes 4177920 | tf_op jit(solution)/shard_map/all_gather | solution.py:171
  9.0 349.8 %all-gather.14.cloned.1.call-start = ((), (), s32[]{:S(2)}) async-start(), calls=%async_computation.4 | async-start | bytes 2785280 | tf_op jit(solution)/shard_map/all_gather | solution.py:177
  14.8 11.0 %collective-permute-start.1 = (bf16[320,1,256]{2,0,1:T(8,128)(2,1)S(1)}, bf16[320,1,256]{2,0,1:T(8,128)(2,1)S(1)}, u32[]{:S(2)}, u32[]{:S(2)}) collective-permute-start(bf16[320,1,256]{2,0,1:T(8,128)(2,1)S(1)} %get-tuple-element.593), channel_id=1, source_target_pairs={{0,16},{16,32},{32,48},{48,64},{64,80},{80,96},{96,112},{112,128},... | collective-permute-start | bytes 491528 | tf_op jit(solution)/shard_map/while/body/eval_jaxpr/ppermute | solution.py:14
  14.9 8.6 %collective-permute-start = (bf16[320,1,256]{2,0,1:T(8,128)(2,1)S(1)}, bf16[320,1,256]{2,0,1:T(8,128)(2,1)S(1)}, u32[]{:S(2)}, u32[]{:S(2)}) collective-permute-start(bf16[320,1,256]{2,0,1:T(8,128)(2,1)S(1)} %get-tuple-element.592), channel_id=1, source_target_pairs={{0,16},{16,32},{32,48},{48,64},{64,80},{80,96},{96,112},{112,128},... | collective-permute-start | bytes 491528 | tf_op jit(solution)/shard_map/while/body/eval_jaxpr/ppermute | solution.py:14
  16.6 15.0 %collective-permute-start.2 = (f32[320,1,256]{2,0,1:T(8,128)S(1)}, f32[320,1,256]{2,0,1:T(8,128)S(1)}, u32[]{:S(2)}, u32[]{:S(2)}) collective-permute-start(f32[320,1,256]{2,0,1:T(8,128)S(1)} %broadcast_select_fusion.4), channel_id=1, source_target_pairs={{0,16},{16,32},{32,48},{48,64},{64,80},{80,96},{96,112},{112,128},... | collective-permute-start | bytes 983048 | tf_op jit(solution)/shard_map/while/body/eval_jaxpr/ppermute | solution.py:14
  16.7 13.9 %collective-permute-start.3 = (f32[320,1,256]{2,0,1:T(8,128)S(1)}, f32[320,1,256]{2,0,1:T(8,128)S(1)}, u32[]{:S(2)}, u32[]{:S(2)}) collective-permute-start(f32[320,1,256]{2,0,1:T(8,128)S(1)} %broadcast_select_fusion.5), channel_id=1, source_target_pairs={{0,16},{16,32},{32,48},{48,64},{64,80},{80,96},{96,112},{112,128},... | collective-permute-start | bytes 983048 | tf_op jit(solution)/shard_map/while/body/eval_jaxpr/ppermute | solution.py:14
  31.7 11.0 %collective-permute-start.1 = (bf16[320,1,256]{2,0,1:T(8,128)(2,1)S(1)}, bf16[320,1,256]{2,0,1:T(8,128)(2,1)S(1)}, u32[]{:S(2)}, u32[]{:S(2)}) collective-permute-start(bf16[320,1,256]{2,0,1:T(8,128)(2,1)S(1)} %get-tuple-element.593), channel_id=1, source_target_pairs={{0,16},{16,32},{32,48},{48,64},{64,80},{80,96},{96,112},{112,128},... | collective-permute-start | bytes 491528 | tf_op jit(solution)/shard_map/while/body/eval_jaxpr/ppermute | solution.py:14
  31.8 8.6 %collective-permute-start = (bf16[320,1,256]{2,0,1:T(8,128)(2,1)S(1)}, bf16[320,1,256]{2,0,1:T(8,128)(2,1)S(1)}, u32[]{:S(2)}, u32[]{:S(2)}) collective-permute-start(bf16[320,1,256]{2,0,1:T(8,128)(2,1)S(1)} %get-tuple-element.592), channel_id=1, source_target_pairs={{0,16},{16,32},{32,48},{48,64},{64,80},{80,96},{96,112},{112,128},... | collective-permute-start | bytes 491528 | tf_op jit(solution)/shard_map/while/body/eval_jaxpr/ppermute | solution.py:14
  31.9 16.4 %collective-permute-start.2 = (f32[320,1,256]{2,0,1:T(8,128)S(1)}, f32[320,1,256]{2,0,1:T(8,128)S(1)}, u32[]{:S(2)}, u32[]{:S(2)}) collective-permute-start(f32[320,1,256]{2,0,1:T(8,128)S(1)} %broadcast_select_fusion.4), channel_id=1, source_target_pairs={{0,16},{16,32},{32,48},{48,64},{64,80},{80,96},{96,112},{112,128},... | collective-permute-start | bytes 983048 | tf_op jit(solution)/shard_map/while/body/eval_jaxpr/ppermute | solution.py:14
  32.0 15.4 %collective-permute-start.3 = (f32[320,1,256]{2,0,1:T(8,128)S(1)}, f32[320,1,256]{2,0,1:T(8,128)S(1)}, u32[]{:S(2)}, u32[]{:S(2)}) collective-permute-start(f32[320,1,256]{2,0,1:T(8,128)S(1)} %broadcast_select_fusion.5), channel_id=1, source_target_pairs={{0,16},{16,32},{32,48},{48,64},{64,80},{80,96},{96,112},{112,128},... | collective-permute-start | bytes 983048 | tf_op jit(solution)/shard_map/while/body/eval_jaxpr/ppermute | solution.py:14
  48.5 11.0 %collective-permute-start.1 = (bf16[320,1,256]{2,0,1:T(8,128)(2,1)S(1)}, bf16[320,1,256]{2,0,1:T(8,128)(2,1)S(1)}, u32[]{:S(2)}, u32[]{:S(2)}) collective-permute-start(bf16[320,1,256]{2,0,1:T(8,128)(2,1)S(1)} %get-tuple-element.593), channel_id=1, source_target_pairs={{0,16},{16,32},{32,48},{48,64},{64,80},{80,96},{96,112},{112,128},... | collective-permute-start | bytes 491528 | tf_op jit(solution)/shard_map/while/body/eval_jaxpr/ppermute | solution.py:14
  48.5 8.6 %collective-permute-start = (bf16[320,1,256]{2,0,1:T(8,128)(2,1)S(1)}, bf16[320,1,256]{2,0,1:T(8,128)(2,1)S(1)}, u32[]{:S(2)}, u32[]{:S(2)}) collective-permute-start(bf16[320,1,256]{2,0,1:T(8,128)(2,1)S(1)} %get-tuple-element.592), channel_id=1, source_target_pairs={{0,16},{16,32},{32,48},{48,64},{64,80},{80,96},{96,112},{112,128},... | collective-permute-start | bytes 491528 | tf_op jit(solution)/shard_map/while/body/eval_jaxpr/ppermute | solution.py:14
  48.7 16.4 %collective-permute-start.2 = (f32[320,1,256]{2,0,1:T(8,128)S(1)}, f32[320,1,256]{2,0,1:T(8,128)S(1)}, u32[]{:S(2)}, u32[]{:S(2)}) collective-permute-start(f32[320,1,256]{2,0,1:T(8,128)S(1)} %broadcast_select_fusion.4), channel_id=1, source_target_pairs={{0,16},{16,32},{32,48},{48,64},{64,80},{80,96},{96,112},{112,128},... | collective-permute-start | bytes 983048 | tf_op jit(solution)/shard_map/while/body/eval_jaxpr/ppermute | solution.py:14
  48.8 15.4 %collective-permute-start.3 = (f32[320,1,256]{2,0,1:T(8,128)S(1)}, f32[320,1,256]{2,0,1:T(8,128)S(1)}, u32[]{:S(2)}, u32[]{:S(2)}) collective-permute-start(f32[320,1,256]{2,0,1:T(8,128)S(1)} %broadcast_select_fusion.5), channel_id=1, source_target_pairs={{0,16},{16,32},{32,48},{48,64},{64,80},{80,96},{96,112},{112,128},... | collective-permute-start | bytes 983048 | tf_op jit(solution)/shard_map/while/body/eval_jaxpr/ppermute | solution.py:14
  65.2 11.1 %collective-permute-start.1 = (bf16[320,1,256]{2,0,1:T(8,128)(2,1)S(1)}, bf16[320,1,256]{2,0,1:T(8,128)(2,1)S(1)}, u32[]{:S(2)}, u32[]{:S(2)}) collective-permute-start(bf16[320,1,256]{2,0,1:T(8,128)(2,1)S(1)} %get-tuple-element.593), channel_id=1, source_target_pairs={{0,16},{16,32},{32,48},{48,64},{64,80},{80,96},{96,112},{112,128},... | collective-permute-start | bytes 491528 | tf_op jit(solution)/shard_map/while/body/eval_jaxpr/ppermute | solution.py:14
  65.3 8.7 %collective-permute-start = (bf16[320,1,256]{2,0,1:T(8,128)(2,1)S(1)}, bf16[320,1,256]{2,0,1:T(8,128)(2,1)S(1)}, u32[]{:S(2)}, u32[]{:S(2)}) collective-permute-start(bf16[320,1,256]{2,0,1:T(8,128)(2,1)S(1)} %get-tuple-element.592), channel_id=1, source_target_pairs={{0,16},{16,32},{32,48},{48,64},{64,80},{80,96},{96,112},{112,128},... | collective-permute-start | bytes 491528 | tf_op jit(solution)/shard_map/while/body/eval_jaxpr/ppermute | solution.py:14
  65.4 16.5 %collective-permute-start.2 = (f32[320,1,256]{2,0,1:T(8,128)S(1)}, f32[320,1,256]{2,0,1:T(8,128)S(1)}, u32[]{:S(2)}, u32[]{:S(2)}) collective-permute-start(f32[320,1,256]{2,0,1:T(8,128)S(1)} %broadcast_select_fusion.4), channel_id=1, source_target_pairs={{0,16},{16,32},{32,48},{48,64},{64,80},{80,96},{96,112},{112,128},... | collective-permute-start | bytes 983048 | tf_op jit(solution)/shard_map/while/body/eval_jaxpr/ppermute | solution.py:14
  65.6 15.5 %collective-permute-start.3 = (f32[320,1,256]{2,0,1:T(8,128)S(1)}, f32[320,1,256]{2,0,1:T(8,128)S(1)}, u32[]{:S(2)}, u32[]{:S(2)}) collective-permute-start(f32[320,1,256]{2,0,1:T(8,128)S(1)} %broadcast_select_fusion.5), channel_id=1, source_target_pairs={{0,16},{16,32},{32,48},{48,64},{64,80},{80,96},{96,112},{112,128},... | collective-permute-start | bytes 983048 | tf_op jit(solution)/shard_map/while/body/eval_jaxpr/ppermute | solution.py:14
  82.1 11.1 %collective-permute-start.1 = (bf16[320,1,256]{2,0,1:T(8,128)(2,1)S(1)}, bf16[320,1,256]{2,0,1:T(8,128)(2,1)S(1)}, u32[]{:S(2)}, u32[]{:S(2)}) collective-permute-start(bf16[320,1,256]{2,0,1:T(8,128)(2,1)S(1)} %get-tuple-element.593), channel_id=1, source_target_pairs={{0,16},{16,32},{32,48},{48,64},{64,80},{80,96},{96,112},{112,128},... | collective-permute-start | bytes 491528 | tf_op jit(solution)/shard_map/while/body/eval_jaxpr/ppermute | solution.py:14
  82.2 8.7 %collective-permute-start = (bf16[320,1,256]{2,0,1:T(8,128)(2,1)S(1)}, bf16[320,1,256]{2,0,1:T(8,128)(2,1)S(1)}, u32[]{:S(2)}, u32[]{:S(2)}) collective-permute-start(bf16[320,1,256]{2,0,1:T(8,128)(2,1)S(1)} %get-tuple-element.592), channel_id=1, source_target_pairs={{0,16},{16,32},{32,48},{48,64},{64,80},{80,96},{96,112},{112,128},... | collective-permute-start | bytes 491528 | tf_op jit(solution)/shard_map/while/body/eval_jaxpr/ppermute | solution.py:14
  82.3 16.5 %collective-permute-start.2 = (f32[320,1,256]{2,0,1:T(8,128)S(1)}, f32[320,1,256]{2,0,1:T(8,128)S(1)}, u32[]{:S(2)}, u32[]{:S(2)}) collective-permute-start(f32[320,1,256]{2,0,1:T(8,128)S(1)} %broadcast_select_fusion.4), channel_id=1, source_target_pairs={{0,16},{16,32},{32,48},{48,64},{64,80},{80,96},{96,112},{112,128},... | collective-permute-start | bytes 983048 | tf_op jit(solution)/shard_map/while/body/eval_jaxpr/ppermute | solution.py:14
  82.4 15.5 %collective-permute-start.3 = (f32[320,1,256]{2,0,1:T(8,128)S(1)}, f32[320,1,256]{2,0,1:T(8,128)S(1)}, u32[]{:S(2)}, u32[]{:S(2)}) collective-permute-start(f32[320,1,256]{2,0,1:T(8,128)S(1)} %broadcast_select_fusion.5), channel_id=1, source_target_pairs={{0,16},{16,32},{32,48},{48,64},{64,80},{80,96},{96,112},{112,128},... | collective-permute-start | bytes 983048 | tf_op jit(solution)/shard_map/while/body/eval_jaxpr/ppermute | solution.py:14
  98.9 11.1 %collective-permute-start.1 = (bf16[320,1,256]{2,0,1:T(8,128)(2,1)S(1)}, bf16[320,1,256]{2,0,1:T(8,128)(2,1)S(1)}, u32[]{:S(2)}, u32[]{:S(2)}) collective-permute-start(bf16[320,1,256]{2,0,1:T(8,128)(2,1)S(1)} %get-tuple-element.593), channel_id=1, source_target_pairs={{0,16},{16,32},{32,48},{48,64},{64,80},{80,96},{96,112},{112,128},... | collective-permute-start | bytes 491528 | tf_op jit(solution)/shard_map/while/body/eval_jaxpr/ppermute | solution.py:14
  99.0 8.7 %collective-permute-start = (bf16[320,1,256]{2,0,1:T(8,128)(2,1)S(1)}, bf16[320,1,256]{2,0,1:T(8,128)(2,1)S(1)}, u32[]{:S(2)}, u32[]{:S(2)}) collective-permute-start(bf16[320,1,256]{2,0,1:T(8,128)(2,1)S(1)} %get-tuple-element.592), channel_id=1, source_target_pairs={{0,16},{16,32},{32,48},{48,64},{64,80},{80,96},{96,112},{112,128},... | collective-permute-start | bytes 491528 | tf_op jit(solution)/shard_map/while/body/eval_jaxpr/ppermute | solution.py:14
  99.2 16.5 %collective-permute-start.2 = (f32[320,1,256]{2,0,1:T(8,128)S(1)}, f32[320,1,256]{2,0,1:T(8,128)S(1)}, u32[]{:S(2)}, u32[]{:S(2)}) collective-permute-start(f32[320,1,256]{2,0,1:T(8,128)S(1)} %broadcast_select_fusion.4), channel_id=1, source_target_pairs={{0,16},{16,32},{32,48},{48,64},{64,80},{80,96},{96,112},{112,128},... | collective-permute-start | bytes 983048 | tf_op jit(solution)/shard_map/while/body/eval_jaxpr/ppermute | solution.py:14
  99.3 15.5 %collective-permute-start.3 = (f32[320,1,256]{2,0,1:T(8,128)S(1)}, f32[320,1,256]{2,0,1:T(8,128)S(1)}, u32[]{:S(2)}, u32[]{:S(2)}) collective-permute-start(f32[320,1,256]{2,0,1:T(8,128)S(1)} %broadcast_select_fusion.5), channel_id=1, source_target_pairs={{0,16},{16,32},{32,48},{48,64},{64,80},{80,96},{96,112},{112,128},... | collective-permute-start | bytes 983048 | tf_op jit(solution)/shard_map/while/body/eval_jaxpr/ppermute | solution.py:14
  115.8 11.0 %collective-permute-start.1 = (bf16[320,1,256]{2,0,1:T(8,128)(2,1)S(1)}, bf16[320,1,256]{2,0,1:T(8,128)(2,1)S(1)}, u32[]{:S(2)}, u32[]{:S(2)}) collective-permute-start(bf16[320,1,256]{2,0,1:T(8,128)(2,1)S(1)} %get-tuple-element.593), channel_id=1, source_target_pairs={{0,16},{16,32},{32,48},{48,64},{64,80},{80,96},{96,112},{112,128},... | collective-permute-start | bytes 491528 | tf_op jit(solution)/shard_map/while/body/eval_jaxpr/ppermute | solution.py:14
  115.9 8.6 %collective-permute-start = (bf16[320,1,256]{2,0,1:T(8,128)(2,1)S(1)}, bf16[320,1,256]{2,0,1:T(8,128)(2,1)S(1)}, u32[]{:S(2)}, u32[]{:S(2)}) collective-permute-start(bf16[320,1,256]{2,0,1:T(8,128)(2,1)S(1)} %get-tuple-element.592), channel_id=1, source_target_pairs={{0,16},{16,32},{32,48},{48,64},{64,80},{80,96},{96,112},{112,128},... | collective-permute-start | bytes 491528 | tf_op jit(solution)/shard_map/while/body/eval_jaxpr/ppermute | solution.py:14
  116.0 16.4 %collective-permute-start.2 = (f32[320,1,256]{2,0,1:T(8,128)S(1)}, f32[320,1,256]{2,0,1:T(8,128)S(1)}, u32[]{:S(2)}, u32[]{:S(2)}) collective-permute-start(f32[320,1,256]{2,0,1:T(8,128)S(1)} %broadcast_select_fusion.4), channel_id=1, source_target_pairs={{0,16},{16,32},{32,48},{48,64},{64,80},{80,96},{96,112},{112,128},... | collective-permute-start | bytes 983048 | tf_op jit(solution)/shard_map/while/body/eval_jaxpr/ppermute | solution.py:14
  116.1 15.4 %collective-permute-start.3 = (f32[320,1,256]{2,0,1:T(8,128)S(1)}, f32[320,1,256]{2,0,1:T(8,128)S(1)}, u32[]{:S(2)}, u32[]{:S(2)}) collective-permute-start(f32[320,1,256]{2,0,1:T(8,128)S(1)} %broadcast_select_fusion.5), channel_id=1, source_target_pairs={{0,16},{16,32},{32,48},{48,64},{64,80},{80,96},{96,112},{112,128},... | collective-permute-start | bytes 983048 | tf_op jit(solution)/shard_map/while/body/eval_jaxpr/ppermute | solution.py:14
  132.5 11.0 %collective-permute-start.1 = (bf16[320,1,256]{2,0,1:T(8,128)(2,1)S(1)}, bf16[320,1,256]{2,0,1:T(8,128)(2,1)S(1)}, u32[]{:S(2)}, u32[]{:S(2)}) collective-permute-start(bf16[320,1,256]{2,0,1:T(8,128)(2,1)S(1)} %get-tuple-element.593), channel_id=1, source_target_pairs={{0,16},{16,32},{32,48},{48,64},{64,80},{80,96},{96,112},{112,128},... | collective-permute-start | bytes 491528 | tf_op jit(solution)/shard_map/while/body/eval_jaxpr/ppermute | solution.py:14
  132.6 8.6 %collective-permute-start = (bf16[320,1,256]{2,0,1:T(8,128)(2,1)S(1)}, bf16[320,1,256]{2,0,1:T(8,128)(2,1)S(1)}, u32[]{:S(2)}, u32[]{:S(2)}) collective-permute-start(bf16[320,1,256]{2,0,1:T(8,128)(2,1)S(1)} %get-tuple-element.592), channel_id=1, source_target_pairs={{0,16},{16,32},{32,48},{48,64},{64,80},{80,96},{96,112},{112,128},... | collective-permute-start | bytes 491528 | tf_op jit(solution)/shard_map/while/body/eval_jaxpr/ppermute | solution.py:14
  132.8 16.4 %collective-permute-start.2 = (f32[320,1,256]{2,0,1:T(8,128)S(1)}, f32[320,1,256]{2,0,1:T(8,128)S(1)}, u32[]{:S(2)}, u32[]{:S(2)}) collective-permute-start(f32[320,1,256]{2,0,1:T(8,128)S(1)} %broadcast_select_fusion.4), channel_id=1, source_target_pairs={{0,16},{16,32},{32,48},{48,64},{64,80},{80,96},{96,112},{112,128},... | collective-permute-start | bytes 983048 | tf_op jit(solution)/shard_map/while/body/eval_jaxpr/ppermute | solution.py:14
  132.9 15.4 %collective-permute-start.3 = (f32[320,1,256]{2,0,1:T(8,128)S(1)}, f32[320,1,256]{2,0,1:T(8,128)S(1)}, u32[]{:S(2)}, u32[]{:S(2)}) collective-permute-start(f32[320,1,256]{2,0,1:T(8,128)S(1)} %broadcast_select_fusion.5), channel_id=1, source_target_pairs={{0,16},{16,32},{32,48},{48,64},{64,80},{80,96},{96,112},{112,128},... | collective-permute-start | bytes 983048 | tf_op jit(solution)/shard_map/while/body/eval_jaxpr/ppermute | solution.py:14
  149.3 11.0 %collective-permute-start.1 = (bf16[320,1,256]{2,0,1:T(8,128)(2,1)S(1)}, bf16[320,1,256]{2,0,1:T(8,128)(2,1)S(1)}, u32[]{:S(2)}, u32[]{:S(2)}) collective-permute-start(bf16[320,1,256]{2,0,1:T(8,128)(2,1)S(1)} %get-tuple-element.593), channel_id=1, source_target_pairs={{0,16},{16,32},{32,48},{48,64},{64,80},{80,96},{96,112},{112,128},... | collective-permute-start | bytes 491528 | tf_op jit(solution)/shard_map/while/body/eval_jaxpr/ppermute | solution.py:14
  149.4 8.6 %collective-permute-start = (bf16[320,1,256]{2,0,1:T(8,128)(2,1)S(1)}, bf16[320,1,256]{2,0,1:T(8,128)(2,1)S(1)}, u32[]{:S(2)}, u32[]{:S(2)}) collective-permute-start(bf16[320,1,256]{2,0,1:T(8,128)(2,1)S(1)} %get-tuple-element.592), channel_id=1, source_target_pairs={{0,16},{16,32},{32,48},{48,64},{64,80},{80,96},{96,112},{112,128},... | collective-permute-start | bytes 491528 | tf_op jit(solution)/shard_map/while/body/eval_jaxpr/ppermute | solution.py:14
  149.5 16.4 %collective-permute-start.2 = (f32[320,1,256]{2,0,1:T(8,128)S(1)}, f32[320,1,256]{2,0,1:T(8,128)S(1)}, u32[]{:S(2)}, u32[]{:S(2)}) collective-permute-start(f32[320,1,256]{2,0,1:T(8,128)S(1)} %broadcast_select_fusion.4), channel_id=1, source_target_pairs={{0,16},{16,32},{32,48},{48,64},{64,80},{80,96},{96,112},{112,128},... | collective-permute-start | bytes 983048 | tf_op jit(solution)/shard_map/while/body/eval_jaxpr/ppermute | solution.py:14
  149.7 15.4 %collective-permute-start.3 = (f32[320,1,256]{2,0,1:T(8,128)S(1)}, f32[320,1,256]{2,0,1:T(8,128)S(1)}, u32[]{:S(2)}, u32[]{:S(2)}) collective-permute-start(f32[320,1,256]{2,0,1:T(8,128)S(1)} %broadcast_select_fusion.5), channel_id=1, source_target_pairs={{0,16},{16,32},{32,48},{48,64},{64,80},{80,96},{96,112},{112,128},... | collective-permute-start | bytes 983048 | tf_op jit(solution)/shard_map/while/body/eval_jaxpr/ppermute | solution.py:14
  166.1 11.0 %collective-permute-start.1 = (bf16[320,1,256]{2,0,1:T(8,128)(2,1)S(1)}, bf16[320,1,256]{2,0,1:T(8,128)(2,1)S(1)}, u32[]{:S(2)}, u32[]{:S(2)}) collective-permute-start(bf16[320,1,256]{2,0,1:T(8,128)(2,1)S(1)} %get-tuple-element.593), channel_id=1, source_target_pairs={{0,16},{16,32},{32,48},{48,64},{64,80},{80,96},{96,112},{112,128},... | collective-permute-start | bytes 491528 | tf_op jit(solution)/shard_map/while/body/eval_jaxpr/ppermute | solution.py:14
  166.2 8.6 %collective-permute-start = (bf16[320,1,256]{2,0,1:T(8,128)(2,1)S(1)}, bf16[320,1,256]{2,0,1:T(8,128)(2,1)S(1)}, u32[]{:S(2)}, u32[]{:S(2)}) collective-permute-start(bf16[320,1,256]{2,0,1:T(8,128)(2,1)S(1)} %get-tuple-element.592), channel_id=1, source_target_pairs={{0,16},{16,32},{32,48},{48,64},{64,80},{80,96},{96,112},{112,128},... | collective-permute-start | bytes 491528 | tf_op jit(solution)/shard_map/while/body/eval_jaxpr/ppermute | solution.py:14
  166.3 16.4 %collective-permute-start.2 = (f32[320,1,256]{2,0,1:T(8,128)S(1)}, f32[320,1,256]{2,0,1:T(8,128)S(1)}, u32[]{:S(2)}, u32[]{:S(2)}) collective-permute-start(f32[320,1,256]{2,0,1:T(8,128)S(1)} %broadcast_select_fusion.4), channel_id=1, source_target_pairs={{0,16},{16,32},{32,48},{48,64},{64,80},{80,96},{96,112},{112,128},... | collective-permute-start | bytes 983048 | tf_op jit(solution)/shard_map/while/body/eval_jaxpr/ppermute | solution.py:14
  166.4 15.4 %collective-permute-start.3 = (f32[320,1,256]{2,0,1:T(8,128)S(1)}, f32[320,1,256]{2,0,1:T(8,128)S(1)}, u32[]{:S(2)}, u32[]{:S(2)}) collective-permute-start(f32[320,1,256]{2,0,1:T(8,128)S(1)} %broadcast_select_fusion.5), channel_id=1, source_target_pairs={{0,16},{16,32},{32,48},{48,64},{64,80},{80,96},{96,112},{112,128},... | collective-permute-start | bytes 983048 | tf_op jit(solution)/shard_map/while/body/eval_jaxpr/ppermute | solution.py:14
  182.8 11.0 %collective-permute-start.1 = (bf16[320,1,256]{2,0,1:T(8,128)(2,1)S(1)}, bf16[320,1,256]{2,0,1:T(8,128)(2,1)S(1)}, u32[]{:S(2)}, u32[]{:S(2)}) collective-permute-start(bf16[320,1,256]{2,0,1:T(8,128)(2,1)S(1)} %get-tuple-element.593), channel_id=1, source_target_pairs={{0,16},{16,32},{32,48},{48,64},{64,80},{80,96},{96,112},{112,128},... | collective-permute-start | bytes 491528 | tf_op jit(solution)/shard_map/while/body/eval_jaxpr/ppermute | solution.py:14
  182.9 8.6 %collective-permute-start = (bf16[320,1,256]{2,0,1:T(8,128)(2,1)S(1)}, bf16[320,1,256]{2,0,1:T(8,128)(2,1)S(1)}, u32[]{:S(2)}, u32[]{:S(2)}) collective-permute-start(bf16[320,1,256]{2,0,1:T(8,128)(2,1)S(1)} %get-tuple-element.592), channel_id=1, source_target_pairs={{0,16},{16,32},{32,48},{48,64},{64,80},{80,96},{96,112},{112,128},... | collective-permute-start | bytes 491528 | tf_op jit(solution)/shard_map/while/body/eval_jaxpr/ppermute | solution.py:14
  183.0 16.4 %collective-permute-start.2 = (f32[320,1,256]{2,0,1:T(8,128)S(1)}, f32[320,1,256]{2,0,1:T(8,128)S(1)}, u32[]{:S(2)}, u32[]{:S(2)}) collective-permute-start(f32[320,1,256]{2,0,1:T(8,128)S(1)} %broadcast_select_fusion.4), channel_id=1, source_target_pairs={{0,16},{16,32},{32,48},{48,64},{64,80},{80,96},{96,112},{112,128},... | collective-permute-start | bytes 983048 | tf_op jit(solution)/shard_map/while/body/eval_jaxpr/ppermute | solution.py:14
  183.2 15.4 %collective-permute-start.3 = (f32[320,1,256]{2,0,1:T(8,128)S(1)}, f32[320,1,256]{2,0,1:T(8,128)S(1)}, u32[]{:S(2)}, u32[]{:S(2)}) collective-permute-start(f32[320,1,256]{2,0,1:T(8,128)S(1)} %broadcast_select_fusion.5), channel_id=1, source_target_pairs={{0,16},{16,32},{32,48},{48,64},{64,80},{80,96},{96,112},{112,128},... | collective-permute-start | bytes 983048 | tf_op jit(solution)/shard_map/while/body/eval_jaxpr/ppermute | solution.py:14
  199.6 11.0 %collective-permute-start.1 = (bf16[320,1,256]{2,0,1:T(8,128)(2,1)S(1)}, bf16[320,1,256]{2,0,1:T(8,128)(2,1)S(1)}, u32[]{:S(2)}, u32[]{:S(2)}) collective-permute-start(bf16[320,1,256]{2,0,1:T(8,128)(2,1)S(1)} %get-tuple-element.593), channel_id=1, source_target_pairs={{0,16},{16,32},{32,48},{48,64},{64,80},{80,96},{96,112},{112,128},... | collective-permute-start | bytes 491528 | tf_op jit(solution)/shard_map/while/body/eval_jaxpr/ppermute | solution.py:14
  199.7 8.6 %collective-permute-start = (bf16[320,1,256]{2,0,1:T(8,128)(2,1)S(1)}, bf16[320,1,256]{2,0,1:T(8,128)(2,1)S(1)}, u32[]{:S(2)}, u32[]{:S(2)}) collective-permute-start(bf16[320,1,256]{2,0,1:T(8,128)(2,1)S(1)} %get-tuple-element.592), channel_id=1, source_target_pairs={{0,16},{16,32},{32,48},{48,64},{64,80},{80,96},{96,112},{112,128},... | collective-permute-start | bytes 491528 | tf_op jit(solution)/shard_map/while/body/eval_jaxpr/ppermute | solution.py:14
  199.8 16.4 %collective-permute-start.2 = (f32[320,1,256]{2,0,1:T(8,128)S(1)}, f32[320,1,256]{2,0,1:T(8,128)S(1)}, u32[]{:S(2)}, u32[]{:S(2)}) collective-permute-start(f32[320,1,256]{2,0,1:T(8,128)S(1)} %broadcast_select_fusion.4), channel_id=1, source_target_pairs={{0,16},{16,32},{32,48},{48,64},{64,80},{80,96},{96,112},{112,128},... | collective-permute-start | bytes 983048 | tf_op jit(solution)/shard_map/while/body/eval_jaxpr/ppermute | solution.py:14
  199.9 15.4 %collective-permute-start.3 = (f32[320,1,256]{2,0,1:T(8,128)S(1)}, f32[320,1,256]{2,0,1:T(8,128)S(1)}, u32[]{:S(2)}, u32[]{:S(2)}) collective-permute-start(f32[320,1,256]{2,0,1:T(8,128)S(1)} %broadcast_select_fusion.5), channel_id=1, source_target_pairs={{0,16},{16,32},{32,48},{48,64},{64,80},{80,96},{96,112},{112,128},... | collective-permute-start | bytes 983048 | tf_op jit(solution)/shard_map/while/body/eval_jaxpr/ppermute | solution.py:14
  216.3 11.0 %collective-permute-start.1 = (bf16[320,1,256]{2,0,1:T(8,128)(2,1)S(1)}, bf16[320,1,256]{2,0,1:T(8,128)(2,1)S(1)}, u32[]{:S(2)}, u32[]{:S(2)}) collective-permute-start(bf16[320,1,256]{2,0,1:T(8,128)(2,1)S(1)} %get-tuple-element.593), channel_id=1, source_target_pairs={{0,16},{16,32},{32,48},{48,64},{64,80},{80,96},{96,112},{112,128},... | collective-permute-start | bytes 491528 | tf_op jit(solution)/shard_map/while/body/eval_jaxpr/ppermute | solution.py:14
  216.4 8.6 %collective-permute-start = (bf16[320,1,256]{2,0,1:T(8,128)(2,1)S(1)}, bf16[320,1,256]{2,0,1:T(8,128)(2,1)S(1)}, u32[]{:S(2)}, u32[]{:S(2)}) collective-permute-start(bf16[320,1,256]{2,0,1:T(8,128)(2,1)S(1)} %get-tuple-element.592), channel_id=1, source_target_pairs={{0,16},{16,32},{32,48},{48,64},{64,80},{80,96},{96,112},{112,128},... | collective-permute-start | bytes 491528 | tf_op jit(solution)/shard_map/while/body/eval_jaxpr/ppermute | solution.py:14
  216.6 16.4 %collective-permute-start.2 = (f32[320,1,256]{2,0,1:T(8,128)S(1)}, f32[320,1,256]{2,0,1:T(8,128)S(1)}, u32[]{:S(2)}, u32[]{:S(2)}) collective-permute-start(f32[320,1,256]{2,0,1:T(8,128)S(1)} %broadcast_select_fusion.4), channel_id=1, source_target_pairs={{0,16},{16,32},{32,48},{48,64},{64,80},{80,96},{96,112},{112,128},... | collective-permute-start | bytes 983048 | tf_op jit(solution)/shard_map/while/body/eval_jaxpr/ppermute | solution.py:14
  216.7 15.4 %collective-permute-start.3 = (f32[320,1,256]{2,0,1:T(8,128)S(1)}, f32[320,1,256]{2,0,1:T(8,128)S(1)}, u32[]{:S(2)}, u32[]{:S(2)}) collective-permute-start(f32[320,1,256]{2,0,1:T(8,128)S(1)} %broadcast_select_fusion.5), channel_id=1, source_target_pairs={{0,16},{16,32},{32,48},{48,64},{64,80},{80,96},{96,112},{112,128},... | collective-permute-start | bytes 983048 | tf_op jit(solution)/shard_map/while/body/eval_jaxpr/ppermute | solution.py:14
  233.1 11.0 %collective-permute-start.1 = (bf16[320,1,256]{2,0,1:T(8,128)(2,1)S(1)}, bf16[320,1,256]{2,0,1:T(8,128)(2,1)S(1)}, u32[]{:S(2)}, u32[]{:S(2)}) collective-permute-start(bf16[320,1,256]{2,0,1:T(8,128)(2,1)S(1)} %get-tuple-element.593), channel_id=1, source_target_pairs={{0,16},{16,32},{32,48},{48,64},{64,80},{80,96},{96,112},{112,128},... | collective-permute-start | bytes 491528 | tf_op jit(solution)/shard_map/while/body/eval_jaxpr/ppermute | solution.py:14
  233.3 16.4 %collective-permute-start.2 = (f32[320,1,256]{2,0,1:T(8,128)S(1)}, f32[320,1,256]{2,0,1:T(8,128)S(1)}, u32[]{:S(2)}, u32[]{:S(2)}) collective-permute-start(f32[320,1,256]{2,0,1:T(8,128)S(1)} %broadcast_select_fusion.4), channel_id=1, source_target_pairs={{0,16},{16,32},{32,48},{48,64},{64,80},{80,96},{96,112},{112,128},... | collective-permute-start | bytes 983048 | tf_op jit(solution)/shard_map/while/body/eval_jaxpr/ppermute | solution.py:14
  233.4 15.4 %collective-permute-start.3 = (f32[320,1,256]{2,0,1:T(8,128)S(1)}, f32[320,1,256]{2,0,1:T(8,128)S(1)}, u32[]{:S(2)}, u32[]{:S(2)}) collective-permute-start(f32[320,1,256]{2,0,1:T(8,128)S(1)} %broadcast_select_fusion.5), channel_id=1, source_target_pairs={{0,16},{16,32},{32,48},{48,64},{64,80},{80,96},{96,112},{112,128},... | collective-permute-start | bytes 983048 | tf_op jit(solution)/shard_map/while/body/eval_jaxpr/ppermute | solution.py:14
  249.9 11.0 %collective-permute-start.1 = (bf16[320,1,256]{2,0,1:T(8,128)(2,1)S(1)}, bf16[320,1,256]{2,0,1:T(8,128)(2,1)S(1)}, u32[]{:S(2)}, u32[]{:S(2)}) collective-permute-start(bf16[320,1,256]{2,0,1:T(8,128)(2,1)S(1)} %get-tuple-element.593), channel_id=1, source_target_pairs={{0,16},{16,32},{32,48},{48,64},{64,80},{80,96},{96,112},{112,128},... | collective-permute-start | bytes 491528 | tf_op jit(solution)/shard_map/while/body/eval_jaxpr/ppermute | solution.py:14
  250.1 16.4 %collective-permute-start.2 = (f32[320,1,256]{2,0,1:T(8,128)S(1)}, f32[320,1,256]{2,0,1:T(8,128)S(1)}, u32[]{:S(2)}, u32[]{:S(2)}) collective-permute-start(f32[320,1,256]{2,0,1:T(8,128)S(1)} %broadcast_select_fusion.4), channel_id=1, source_target_pairs={{0,16},{16,32},{32,48},{48,64},{64,80},{80,96},{96,112},{112,128},... | collective-permute-start | bytes 983048 | tf_op jit(solution)/shard_map/while/body/eval_jaxpr/ppermute | solution.py:14
  250.2 15.4 %collective-permute-start.3 = (f32[320,1,256]{2,0,1:T(8,128)S(1)}, f32[320,1,256]{2,0,1:T(8,128)S(1)}, u32[]{:S(2)}, u32[]{:S(2)}) collective-permute-start(f32[320,1,256]{2,0,1:T(8,128)S(1)} %broadcast_select_fusion.5), channel_id=1, source_target_pairs={{0,16},{16,32},{32,48},{48,64},{64,80},{80,96},{96,112},{112,128},... | collective-permute-start | bytes 983048 | tf_op jit(solution)/shard_map/while/body/eval_jaxpr/ppermute | solution.py:14
  266.6 8.7 %collective-permute-start.5 = (f32[320,1,256]{2,0,1:T(8,128)S(1)}, f32[320,1,256]{2,0,1:T(8,128)S(1)}, u32[]{:S(2)}, u32[]{:S(2)}) collective-permute-start(f32[320,1,256]{2,0,1:T(8,128)S(1)} %get-tuple-element.369), channel_id=1, source_target_pairs={{0,16},{16,32},{32,48},{48,64},{64,80},{80,96},{96,112},{112,128},... | collective-permute-start | bytes 983048 | tf_op jit(solution)/shard_map/ppermute | solution.py:14
  276.3 108.7 %all-gather.10.cloned.1.call-start = ((), (), s32[]{:S(2)}) async-start(), calls=%async_computation.2 | async-start | bytes 2785280 | tf_op jit(solution)/shard_map/all_gather | solution.py:175
  277.5 147.3 %all-gather.12.cloned.1.call-start = ((), (), s32[]{:S(2)}) async-start(), calls=%async_computation.3 | async-start | bytes 2785280 | tf_op jit(solution)/shard_map/all_gather | solution.py:176
  277.6 8.7 %collective-permute-start.4 = (f32[320,1,256]{2,0,1:T(8,128)S(1)}, f32[320,1,256]{2,0,1:T(8,128)S(1)}, u32[]{:S(2)}, u32[]{:S(2)}) collective-permute-start(f32[320,1,256]{2,0,1:T(8,128)S(1)} %get-tuple-element.368), channel_id=1, source_target_pairs={{0,16},{16,32},{32,48},{48,64},{64,80},{80,96},{96,112},{112,128},... | collective-permute-start | bytes 983048 | tf_op jit(solution)/shard_map/ppermute | solution.py:14
  (36 other events, 877.7 us)
Sparse Core Ops, SparseCore 0:
  11.2 132.1 all-gather.7
  276.4 69.3 all-gather.13
  348.2 36.7 all-gather.9
  387.3 37.4 all-gather.11
where the time goes:
time: 440 us; the launch traced here: 436 us
  waiting for transfers between devices  198 us (45%)
  matrix products  84.8 us (19%)
  blocking collectives  60.3 us (14%)
  local copies, waits for them, and re-layouts  47.5 us (11%)
  between operations  15.3 us (3%)
  loops' own time  13.1 us (3%)
  starting transfers between devices  9.29 us (2%)
  other arithmetic  7.74 us (2%)
    ppermute x62, waiting for transfers between devices, from_behind(): lax.ppermute(shard, axis, [(i, (i + by) % devices) for i in range(devices)])  140 us
    all_to_all x1, blocking collectives, body(): lax.all_to_all(full_rows, 'ctx', split_axis=1, concat_axis=0, tiled=True)  60.3 us
    all_gather x1, waiting for transfers between devices, body(): lax.all_gather(grad_key, 'ctx', axis=0, tiled=True)  36 us
    all_gather x1, waiting for transfers between devices, body(): lax.all_gather(grad_query, 'ctx', axis=0, tiled=True)  22.3 us
    dynamic_slice x15, local copies, waits for them, and re-layouts, visit_keys(): block_order[source]  19 us
    dot_general x16, matrix products, block_grads(): jnp.einsum('qhd,khd->hqk', queries[..., :HALF], key_rows[..., :HALF], pre...  18.6 us
    dot_general x16, matrix products, block_grads(): jnp.einsum('qhd,khd->hqk', queries[..., HALF:], key_rows[..., HALF:], pre...  18.5 us
    dot_general x16, matrix products, block_grads(): jnp.einsum('hqk,qhd->khd', mixture, grad_rows, preferred_element_type=jnp...  15.1 us
  transfers between devices with their start and end apart: 66, of which 34 were waited for; matrix products, arithmetic and copies ran while one was open for 29% of the time, Pallas kernels for 0%

commit v1 on v0

v1 whole, which is shorter than its diff:
```python
import functools
import math

import jax
import jax.numpy as jnp
from jax import lax
from jax.experimental import pallas as pl
from jax.experimental.pallas import tpu as pltpu
from jax.sharding import PartitionSpec as P

HALF = 128
WIDE = 256
LEN = 320
PAIR = 640
ALL = 1280
SCALE = 0.08838834764831845
LOG2E = 1.4426950408889634
F32 = jnp.float32
BF16 = jnp.bfloat16
MESH = pl.DeviceIdType.MESH

NN = (((1,), (0,)), ((), ()))
NT = (((1,), (1,)), ((), ()))


def dot(a, b, dims=NN):
    return lax.dot_general(a, b, dims, preferred_element_type=F32)


def kernel(
    x_ref, q_ref, k_ref, v_ref, o1_ref, o2_ref, g_ref, lse_ref, lam_ref, order_ref,
    dq_out, dk_out, dv_out, w_out,
    qb, gb, st, stp, kb, vb, kt, dkv, dqt,
    dqs, dqr, sib_s, sib_r, par_s, par_r, gw, lb, lt, ws, wr,
    send, recv, zsend, zrecv, lsend, lrecv, wsend, wrecv,
):
    c = lax.axis_index("ctx")
    h = lax.axis_index("head")
    yl, x, k = c // 8, (c // 2) % 4, c % 2
    yh, z = h // 8, h % 8

    def dev(yl_, x_, k_, yh_, z_):
        return ((yl_ * 4 + x_) * 2 + k_, yh_ * 8 + z_)

    def xdev(d):
        return dev(yl, (x + d) % 4, k, yh, z)

    def zdev(d):
        return dev(yl, x, k, yh, (z + d) % 8)

    sib = dev(yl, x, 1 - k, yh, z)
    par = dev(1 - yl, x, k, yh, z)

    barrier = pltpu.get_barrier_semaphore()
    partners = [xdev(1), xdev(2), xdev(3), zdev(1), zdev(7)]
    for a in range(2):
        for b in range(2):
            for e in range(2):
                if a + b + e > 0:
                    partners.append(dev((yl + a) % 2, x, (k + b) % 2, (yh + e) % 2, z))
    for p in partners:
        pl.semaphore_signal(barrier, inc=1, device_id=p, device_id_type=MESH)
    pl.semaphore_wait(barrier, len(partners))

    used = [0]

    def remote(src, dst, to):
        i = used[0]
        used[0] += 1
        return pltpu.make_async_remote_copy(
            src_ref=src, dst_ref=dst, send_sem=send.at[i], recv_sem=recv.at[i],
            device_id=to, device_id_type=MESH,
        )

    pending = []

    def go(cp):
        cp.start()
        pending.append(cp)
        return cp

    t_own = yl * 2 + k
    holder = k == z % 2
    home = yh == yl

    def l_copy(e):
        return pltpu.make_async_remote_copy(
            src_ref=x_ref, dst_ref=lb.at[t_own], send_sem=lsend.at[e], recv_sem=lrecv.at[t_own],
            device_id=dev(yh, x, z % 2, (yh + e) % 2, z), device_id_type=MESH,
        )

    mine = jnp.logical_and(holder, home)
    l_local = pltpu.make_async_copy(x_ref, lb.at[t_own], lrecv.at[t_own])

    @pl.when(mine)
    def _():
        l_local.start()

    @pl.when(jnp.logical_not(mine))
    def _():
        l_copy(0).start()

    l_copy(1).start()

    gq = [go(remote(q_ref, qb.at[s], xdev(d))) for s, d in ((1, 1), (2, 3))]
    gg = [go(remote(g_ref, gb.at[s], xdev(d))) for s, d in ((1, 1), (2, 3))]
    gk = [go(remote(k_ref, kb.at[1], sib)), go(remote(k_ref, kb.at[2], par))]
    gv = [go(remote(v_ref, vb.at[1], sib)), go(remote(v_ref, vb.at[2], par))]
    gq.append(go(remote(q_ref, qb.at[3], xdev(2))))
    gg.append(go(remote(g_ref, gb.at[3], xdev(2))))

    gf = g_ref[...].astype(F32)
    ones = jnp.ones((16, WIDE), BF16)

    def row_sums(o_ref):
        prod = gf * o_ref[...].astype(F32)
        hi = prod.astype(BF16)
        lo = (prod - hi.astype(F32)).astype(BF16)
        return (dot(ones, hi, NT) + dot(ones, lo, NT))[0:1]

    lam = jnp.full((1, LEN), lam_ref[0], F32)
    st[0, 0:1, :] = lse_ref[0] * LOG2E
    st[0, 1:2, :] = lse_ref[1] * LOG2E - jnp.log(lam) * LOG2E
    st[0, 2:3, :] = row_sums(o1_ref)
    st[0, 3:4, :] = row_sums(o2_ref)
    st[0, 4:8, :] = jnp.zeros((4, LEN), F32)
    gs = [go(remote(st.at[0], st.at[s], xdev(d))) for s, d in ((1, 1), (2, 3), (3, 2))]

    qb[0] = q_ref[...]
    gb[0] = g_ref[...]
    kb[0] = k_ref[...]
    vb[0] = v_ref[...]

    eye = (
        lax.broadcasted_iota(jnp.int32, (LEN, LEN), 0)
        == lax.broadcasted_iota(jnp.int32, (LEN, LEN), 1)
    ).astype(F32).astype(BF16)
    eye_wide = eye[0:WIDE, 0:WIDE]

    def transpose_keys(j):
        kt[j] = dot(eye_wide, kb[j], NT).astype(BF16)

    transpose_keys(0)

    def z_copy(src_z, half, way, event):
        rows = pl.ds(half * 160, 160)
        ref = lt.at[(src_z % 8) // 2, rows]
        return pltpu.make_async_remote_copy(
            src_ref=ref, dst_ref=ref,
            send_sem=zsend.at[way, event, half], recv_sem=zrecv.at[way, event, half],
            device_id=zdev(1 if way == 0 else 7), device_id_type=MESH,
        )

    @pl.when(holder)
    def _():
        for t in range(4):
            pltpu.make_async_copy(x_ref, lb.at[t], lrecv.at[t]).wait()
        lt[z // 2] = dot(eye, lb[...].reshape(ALL, LEN), NT).astype(BF16)
        for half in range(2):
            for way in range(2):
                z_copy(z, half, way, 0).start()

    def z_wait(event, half, way):
        z_copy(z, half, way, event).wait_recv()

    def arrived(way, far):
        return z - far + 8 if way == 0 else z + far

    def relay_near(half):
        @pl.when(jnp.logical_not(holder))
        def _():
            for way in range(2):
                z_wait(0, half, way)
                z_copy(arrived(way, 1), half, way, 0).start()

    def relay_mid(half):
        @pl.when(holder)
        def _():
            for way in range(2):
                z_wait(0, half, way)
                z_copy(arrived(way, 2), half, way, 1).start()

    def relay_far(half):
        @pl.when(jnp.logical_not(holder))
        def _():
            for way in range(2):
                z_wait(1, half, way)
                if way == half:
                    z_copy(arrived(way, 3), half, way, 1).start()

    def finish_z():
        @pl.when(holder)
        def _():
            for way in range(2):
                z_wait(1, way, way)

    def block(yl_, x_, k_):
        return order_ref[(yl_ * 4 + x_) * 2 + k_]

    q_pos = [block(yl, (x + d) % 4, k) for d in (0, 3, 1, 2)]
    first = lax.broadcasted_iota(jnp.int32, (1, PAIR), 1) < LEN

    def key_pos(j):
        return block((yl + j // 2) % 2, x, (k + j % 2) % 2)

    def attend(p, j, diagonal, fresh_keys, fresh_queries):
        rows = slice(p * PAIR, (p + 1) * PAIR)
        qs = qb[2 * p : 2 * p + 2].reshape(PAIR, WIDE)
        grads = gb[2 * p : 2 * p + 2].reshape(PAIR, WIDE)
        keys = kb[j]
        pos = key_pos(j)
        hide = jnp.where(
            first,
            jnp.where(pos > q_pos[2 * p], 1e30, 0.0),
            jnp.where(pos > q_pos[2 * p + 1], 1e30, 0.0),
        )
        stats = stp[p]
        up = dot(vb[j], grads, NT)
        p1 = jnp.exp2(dot(keys[:, :HALF], qs[:, :HALF], NT) * (SCALE * LOG2E) - (stats[0:1] + hide))
        p2 = jnp.exp2(dot(keys[:, HALF:], qs[:, HALF:], NT) * (SCALE * LOG2E) - (stats[1:2] + hide))
        if diagonal:
            key_row = lax.broadcasted_iota(jnp.int32, (LEN, PAIR), 0)
            query_col = lax.broadcasted_iota(jnp.int32, (LEN, PAIR), 1)
            seen = key_row <= query_col
            p1 = jnp.where(seen, p1, 0.0)
            p2 = jnp.where(seen, p2, 0.0)
        s1 = (p1 * (up - stats[2:3])).astype(BF16)
        s2 = (p2 * (up - stats[3:4])).astype(BF16)
        mix = (p1 - p2).astype(BF16)
        dk1 = dot(s1, qs[:, :HALF])
        dk2 = dot(s2, qs[:, HALF:])
        dv = dot(mix, grads)
        if fresh_keys:
            dkv[j, :, 0:HALF] = dk1
            dkv[j, :, HALF:WIDE] = dk2
            dkv[j, :, WIDE:] = dv
        else:
            dkv[j, :, 0:HALF] += dk1
            dkv[j, :, HALF:WIDE] += dk2
            dkv[j, :, WIDE:] += dv
        dq1 = dot(kt[j, 0:HALF, :], s1)
        dq2 = dot(kt[j, HALF:WIDE, :], s2)
        if fresh_queries:
            dqt[p, 0:HALF] = dq1
            dqt[p, HALF:WIDE] = dq2
        else:
            dqt[p, 0:HALF] += dq1
            dqt[p, HALF:WIDE] += dq2

    def finish_dq(p):
        return dqt[p].T

    def signed(t):
        sign = jnp.where(lax.broadcasted_iota(jnp.int32, (1, WIDE), 1) < HALF, SCALE, -SCALE)
        return t * sign

    gq[0].wait_recv()
    gg[0].wait_recv()
    gs[0].wait_recv()
    stp[0] = jnp.concatenate([st[0], st[1]], axis=1)
    attend(0, 0, True, True, True)
    gk[0].wait_recv()
    gv[0].wait_recv()
    transpose_keys(1)
    gk[1].wait_recv()
    rk = go(remote(kb.at[2], kb.at[3], sib))
    gv[1].wait_recv()
    rv = go(remote(vb.at[2], vb.at[3], sib))
    transpose_keys(2)
    rk.wait_recv()
    rv.wait_recv()
    transpose_keys(3)

    def early(j, carry):
        attend(0, j, False, True, False)
        return carry

    lax.fori_loop(1, 4, early, 0)
    relay_near(0)

    dq_a = finish_dq(0)
    dqs[0] = dq_a[LEN:PAIR].astype(BF16)
    sq = [go(remote(dqs.at[0], dqr.at[0], xdev(3)))]

    for i in (1, 2):
        gq[i].wait_recv()
        gg[i].wait_recv()
        gs[i].wait_recv()
    stp[1] = jnp.concatenate([st[2], st[3]], axis=1)
    dqt[1] = jnp.zeros_like(dqt[1])

    def late(i, carry):
        attend(1, 3 - i, False, False, False)
        return carry

    lax.fori_loop(0, 2, late, 0)
    sib_s[0] = dkv[3].astype(BF16)
    b0 = go(remote(sib_s.at[0], sib_r.at[0], sib))
    relay_near(1)
    b0.wait_recv()
    par_s[...] = (dkv[2] + sib_r[0].astype(F32)).astype(BF16)
    b1 = go(remote(par_s, par_r, par))
    lax.fori_loop(2, 4, late, 0)
    dq_b = finish_dq(1)
    dqs[1] = dq_b[0:LEN].astype(BF16)
    dqs[2] = dq_b[LEN:PAIR].astype(BF16)
    sq.append(go(remote(dqs.at[1], dqr.at[1], xdev(1))))
    sq.append(go(remote(dqs.at[2], dqr.at[2], xdev(2))))
    sib_s[1] = dkv[1].astype(BF16)
    b2 = go(remote(sib_s.at[1], sib_r.at[1], sib))
    relay_mid(0)

    own_rows = pl.ds(pl.multiple_of(t_own * LEN, LEN), LEN)

    def share(i, value, out):
        out[...] = value
        ref = gw.at[i, own_rows]
        ref[...] = value
        return [go(remote(ref, ref, sib)), go(remote(ref, ref, par))]

    par_rows = pl.ds(pl.multiple_of(((1 - yl) * 2 + k) * LEN, LEN), LEN)

    def pass_on(i, copies):
        copies[1].wait_recv()
        ref = gw.at[i, par_rows]
        copies.append(go(remote(ref, ref, sib)))

    for cp in sq:
        cp.wait_recv()
    total = dqt[0].T[0:LEN]
    for i in range(3):
        total = total + dqr[i].astype(F32)
    c0 = share(0, signed(total).astype(BF16), dq_out)

    b1.wait_recv()
    b2.wait_recv()
    total = dkv[0] + sib_r[1].astype(F32) + par_r[...].astype(F32)
    c1 = share(1, signed(total[:, 0:WIDE]).astype(BF16), dk_out)
    c2 = share(2, total[:, WIDE:].astype(BF16), dv_out)
    relay_mid(1)
    pass_on(0, c0)
    relay_far(0)
    pass_on(1, c1)
    relay_far(1)
    pass_on(2, c2)
    finish_z()
    for cps in (c0, c1, c2):
        cps[0].wait_recv()
        cps[2].wait_recv()

    def w_copy(i, r):
        return pltpu.make_async_remote_copy(
            src_ref=ws.at[r - 1, i], dst_ref=wr.at[r - 1, i],
            send_sem=wsend.at[r - 1, i], recv_sem=wrecv.at[r - 1, i],
            device_id=xdev(r), device_id_type=MESH,
        )

    for i in range(3):
        def part(r, carry):
            ws[r - 1, i] = dot(lt[(x + r) % 4], gw[i]).astype(BF16)
            w_copy(i, r).start()
            return carry

        lax.fori_loop(1, 4, part, 0)
    for i in range(3):
        w_out[i] = dot(lt[x], gw[i])
    for i in range(3):
        for r in range(1, 4):
            w_copy(i, r).wait_recv()
        w_out[i] += wr[0, i].astype(F32) + wr[1, i].astype(F32) + wr[2, i].astype(F32)

    for cp in pending:
        cp.wait_send()

    @pl.when(jnp.logical_not(mine))
    def _():
        l_copy(0).wait_send()

    l_copy(1).wait_send()
    for half in range(2):
        for way in range(2):
            z_copy(z, half, way, 0).wait_send()

            @pl.when(jnp.logical_or(holder, way == half))
            def _():
                z_copy(z, half, way, 1).wait_send()

    for i in range(3):
        for r in range(1, 4):
            w_copy(i, r).wait_send()


def body(*args):
    vmem = pl.BlockSpec(memory_space=pltpu.VMEM)
    smem = pl.BlockSpec(memory_space=pltpu.SMEM)
    grad = jax.ShapeDtypeStruct((LEN, WIDE), BF16)
    dma = pltpu.SemaphoreType.DMA
    return pl.pallas_call(
        kernel,
        out_shape=(grad, grad, grad, jax.ShapeDtypeStruct((3, LEN, WIDE), F32)),
        in_specs=[vmem] * 8 + [smem] * 2,
        out_specs=(vmem,) * 4,
        scratch_shapes=[
            pltpu.VMEM((4, LEN, WIDE), BF16),
            pltpu.VMEM((4, LEN, WIDE), BF16),
            pltpu.VMEM((4, 8, LEN), F32),
            pltpu.VMEM((2, 8, PAIR), F32),
            pltpu.VMEM((4, LEN, WIDE), BF16),
            pltpu.VMEM((4, LEN, WIDE), BF16),
            pltpu.VMEM((4, WIDE, LEN), BF16),
            pltpu.VMEM((4, LEN, 2 * WIDE), F32),
            pltpu.VMEM((2, WIDE, PAIR), F32),
            pltpu.VMEM((3, LEN, WIDE), BF16),
            pltpu.VMEM((3, LEN, WIDE), BF16),
            pltpu.VMEM((2, LEN, 2 * WIDE), BF16),
            pltpu.VMEM((2, LEN, 2 * WIDE), BF16),
            pltpu.VMEM((LEN, 2 * WIDE), BF16),
            pltpu.VMEM((LEN, 2 * WIDE), BF16),
            pltpu.VMEM((3, ALL, WIDE), BF16),
            pltpu.VMEM((4, LEN, LEN), BF16),
            pltpu.VMEM((4, LEN, ALL), BF16),
            pltpu.VMEM((3, 3, LEN, WIDE), BF16),
            pltpu.VMEM((3, 3, LEN, WIDE), BF16),
            dma((32,)),
            dma((32,)),
            dma((2, 2, 2)),
            dma((2, 2, 2)),
            dma((2,)),
            dma((4,)),
            dma((3, 3)),
            dma((3, 3)),
        ],
        compiler_params=pltpu.CompilerParams(
            collective_id=0, has_side_effects=True, vmem_limit_bytes=56 * 2**20
        ),
        name="diff_attention_backward",
    )(*args)


def solution(mesh):
    in_specs = (P("ctx", "head"),) * 7 + (P(None, "head", "ctx"), P("head"), P())
    out_specs = (P("ctx", "head"), P("ctx", "head"), P("ctx", "head"), P(None, "ctx", "head"))
    return jax.shard_map(body, mesh=mesh, in_specs=in_specs, out_specs=out_specs, check_vma=False)
```

time: 440 us -> 92.4 us (0.21)
  waiting for transfers between devices: 198 us -> 0 us
  matrix products: 84.8 us -> 0 us
  Pallas kernels: 0 us -> 84.1 us
  blocking collectives: 60.3 us -> 0 us
  local copies, waits for them, and re-layouts: 47.5 us -> 5.81 us
  between operations: 15.3 us -> 1.3 us
  loops' own time: 13.1 us -> 0 us
  starting transfers between devices: 9.29 us -> 0 us
  other arithmetic: 7.74 us -> 0 us
    ppermute x62 -> x0, waiting for transfers between devices: 140 us -> none  [from_behind(): lax.ppermute(shard, axis, [(i, (i + by) % devices) for i in range(devices)])]
    dot_general x131 -> x0, matrix products: 84.8 us -> none  [the longest x16 18.6 us: block_grads(): jnp.einsum('qhd,khd->hqk', queries[..., :HALF], key_rows[..., :HALF], pre...]
    pallas_call x0 -> x1, Pallas kernels: none -> 84.1 us  [body(): pl.pallas_call(kernel, out_shape=(grad, grad, grad, jax.ShapeDtypeStruct(...]
    all_to_all x1 -> x0, blocking collectives: 60.3 us -> none  [body(): lax.all_to_all(full_rows, 'ctx', split_axis=1, concat_axis=0, tiled=True)]
    all_gather x4 -> x0, waiting for transfers between devices: 58.4 us -> none  [the longest x1 36 us: body(): lax.all_gather(grad_key, 'ctx', axis=0, tiled=True)]
    dynamic_slice x16 -> x0, local copies, waits for them, and re-layouts: 20.3 us -> none  [the longest x15 19 us: visit_keys(): block_order[source]]
    another operation x1 -> x0, loops' own time: 13.1 us -> none  [travel(): lax.fori_loop(0, cycle_size - 1, single, (light_part, heavy_part, local_p...]
    all_to_all x2 -> x0, local copies, waits for them, and re-layouts: 11.5 us -> none  [body(): lax.all_to_all(full_rows, 'ctx', split_axis=1, concat_axis=0, tiled=True)]
  transfers between devices with their start and end apart: 66 -> 0, of which waited for: 34 -> 0; matrix products, arithmetic and copies ran while one was open for 29% -> 0% of each run, Pallas kernels for 0% -> 0%
where the time goes in v1:
time: 92.4 us; the launch traced here: 91.2 us
  Pallas kernels  84.1 us (91%)
  local copies, waits for them, and re-layouts  5.81 us (6%)
  between operations  1.3 us (1%)
    pallas_call x1, Pallas kernels, body(): pl.pallas_call(kernel, out_shape=(grad, grad, grad, jax.ShapeDtypeStruct(...  84.1 us
    unnamed x6, local copies, waits for them, and re-layouts  5.81 us

profile of v1, /device:TPU:8, one launch (start us, length us, event | category | flops | bytes accessed | tf_op | source)
XLA Modules:
  0.0 91.2 jit_solution(2079149547989561049)
XLA Ops:
  1.3 84.1 %diff_attention_backward.1 = (bf16[320,256]{1,0:T(8,128)(2,1)}, bf16[320,256]{1,0:T(8,128)(2,1)}, bf16[320,256]{1,0:T(8,128)(2,1)}, f32[3,320,256]{2,1,0:T(8,128)}) custom-call(bf16[320,320]{1,0:T(8,128)(2,1)} %x_ref.1, bf16[320,256]{1,0:T(8,128)(2,1)} %q_ref.1, bf16[320,256]{1,0:T(8,128)(2,1)} %k_ref.1, bf16[320,256]{1,0:T(8,128)(2,1)} %v_ref.1, ...), custom_call_target="tpu_custom_call" | custom-call | tf_op jit(solution)/shard_map/diff_attention_backward/pallas_call | solution.py:398
  85.4 0.0 copy-start
  85.4 1.7 %copy.19 = bf16[320,256]{1,0:T(8,128)(2,1)} copy(bf16[320,256]{1,0:T(8,128)(2,1)} %get-tuple-element.8) | data formatting | bytes 327680
  87.0 1.6 %copy.20 = bf16[320,256]{1,0:T(8,128)(2,1)} copy(bf16[320,256]{1,0:T(8,128)(2,1)} %get-tuple-element.9) | data formatting | bytes 327680
  88.6 1.6 %copy.21 = bf16[320,256]{1,0:T(8,128)(2,1)} copy(bf16[320,256]{1,0:T(8,128)(2,1)} %get-tuple-element.10) | data formatting | bytes 327680
  90.2 0.0 copy-done
  90.2 0.9 %copy.22 = f32[3,320,256]{2,1,0:T(8,128)} copy(f32[3,320,256]{2,1,0:T(8,128)S(1)} %copy-done) | data formatting | bytes 1966080
Async XLA Ops:
  85.4 4.9 %copy-start = (f32[3,320,256]{2,1,0:T(8,128)S(1)}, f32[3,320,256]{2,1,0:T(8,128)}, u32[]{:S(2)}) copy-start(f32[3,320,256]{2,1,0:T(8,128)} %get-tuple-element.11) | copy-start | bytes 2949124

commit v2 on v1

v2 whole, which is shorter than its diff:
```python
import functools
import math

import jax
import jax.numpy as jnp
from jax import lax
from jax.experimental import pallas as pl
from jax.experimental.pallas import tpu as pltpu
from jax.sharding import PartitionSpec as P

HALF = 128
WIDE = 256
LEN = 320
PAIR = 640
TILE = 256
ALL = 1280
SCALE = 0.08838834764831845
LOG2E = 1.4426950408889634
F32 = jnp.float32
BF16 = jnp.bfloat16
MESH = pl.DeviceIdType.MESH

NN = (((1,), (0,)), ((), ()))
NT = (((1,), (1,)), ((), ()))


def dot(a, b, dims=NN):
    return lax.dot_general(a, b, dims, preferred_element_type=F32)


def kernel(
    x_ref, q_ref, k_ref, v_ref, o1_ref, o2_ref, g_ref, lse_ref, lam_ref, order_ref,
    dq_out, dk_out, dv_out, w_out,
    qb, gb, st, stp, kb, vb, kt, dkv, dqt, dqf,
    dqs, dqr, sib_s, sib_r, par_s, par_r, gw, xp, lb, tb, zb, sb, pp, hr, ws, wr,
    send, recv, zsend, zrecv, dsend, drecv, tsend, trecv, lsend, lrecv, hsend, hrecv, wsend, wrecv,
):
    c = lax.axis_index("ctx")
    h = lax.axis_index("head")
    yl, x, k = c // 8, (c // 2) % 4, c % 2
    yh, z = h // 8, h % 8

    def dev(yl_, x_, k_, yh_, z_):
        return ((yl_ * 4 + x_) * 2 + k_, yh_ * 8 + z_)

    def xdev(d):
        return dev(yl, (x + d) % 4, k, yh, z)

    def zdev(d):
        return dev(yl, x, k, yh, (z + d) % 8)

    sib = dev(yl, x, 1 - k, yh, z)
    par = dev(1 - yl, x, k, yh, z)

    barrier = pltpu.get_barrier_semaphore()
    partners = [xdev(1), xdev(2), xdev(3), zdev(1), zdev(7)]
    for a in range(2):
        for b in range(2):
            for e in range(2):
                if a + b + e > 0:
                    partners.append(dev((yl + a) % 2, x, (k + b) % 2, (yh + e) % 2, z))
    for p in partners:
        pl.semaphore_signal(barrier, inc=1, device_id=p, device_id_type=MESH)
    xp[...] = jnp.concatenate([x_ref[0 : LEN // 2], x_ref[LEN // 2 : LEN]], axis=1)
    pl.semaphore_wait(barrier, len(partners))

    used = [0]

    def remote(src, dst, to):
        i = used[0]
        used[0] += 1
        return pltpu.make_async_remote_copy(
            src_ref=src, dst_ref=dst, send_sem=send.at[i], recv_sem=recv.at[i],
            device_id=to, device_id_type=MESH,
        )

    pending = []

    def go(cp):
        cp.start()
        pending.append(cp)
        return cp

    def slot(ref, j):
        return ref.at[pl.ds(j * LEN, LEN)]

    def l_copy(e):
        return pltpu.make_async_remote_copy(
            src_ref=xp, dst_ref=lb.at[k], send_sem=lsend.at[e], recv_sem=lrecv.at[k],
            device_id=dev(yh, x, yl, (yh + e) % 2, z), device_id_type=MESH,
        )

    mine = jnp.logical_and(yh == yl, k == yl)
    l_local = pltpu.make_async_copy(xp, lb.at[k], lrecv.at[k])

    @pl.when(mine)
    def _():
        l_local.start()

    l_copy(1).start()

    @pl.when(jnp.logical_not(mine))
    def _():
        l_copy(0).start()

    q1 = go(remote(q_ref, slot(qb, 1), xdev(1)))
    g2 = go(remote(g_ref, slot(gb, 2), xdev(3)))
    g1 = go(remote(g_ref, slot(gb, 1), xdev(1)))
    q2 = go(remote(q_ref, slot(qb, 2), xdev(3)))
    ks = go(remote(k_ref, slot(kb, 1), sib))
    vs = go(remote(v_ref, slot(vb, 1), sib))

    gf = g_ref[...].astype(F32)
    ones = jnp.ones((16, WIDE), BF16)

    def row_sums(o_ref):
        prod = gf * o_ref[...].astype(F32)
        hi = prod.astype(BF16)
        lo = (prod - hi.astype(F32)).astype(BF16)
        return (dot(ones, hi, NT) + dot(ones, lo, NT))[0:1]

    def position(yl_, x_, k_):
        return order_ref[(yl_ * 4 + x_) * 2 + k_].astype(F32)

    lam = jnp.full((1, LEN), lam_ref[0], F32)
    st[0, 0:1, :] = lse_ref[0] * LOG2E
    st[0, 1:2, :] = lse_ref[1] * LOG2E - jnp.log(lam) * LOG2E
    st[0, 2:3, :] = row_sums(o1_ref)
    st[0, 3:4, :] = row_sums(o2_ref)
    st[0, 4:5, :] = jnp.full((1, LEN), position(yl, x, k), F32)
    st[0, 5:8, :] = jnp.zeros((3, LEN), F32)
    gs = [go(remote(st.at[0], st.at[s], xdev(d))) for s, d in ((1, 1), (2, 3), (3, 2))]

    kp = go(remote(k_ref, slot(kb, 2), par))
    vp = go(remote(v_ref, slot(vb, 2), par))
    qb[0:LEN] = q_ref[...]
    gb[0:LEN] = g_ref[...]
    kb[0:LEN] = k_ref[...]
    vb[0:LEN] = v_ref[...]

    eye = (
        lax.broadcasted_iota(jnp.int32, (LEN, LEN), 0)
        == lax.broadcasted_iota(jnp.int32, (LEN, LEN), 1)
    ).astype(F32).astype(BF16)
    eye_wide = eye[0:WIDE, 0:WIDE]

    match = z % 2 == k
    soon = jnp.where(yh == yl, yl, 1 - yl)
    later = 1 - soon

    def z_copy(src, dst, pair, way):
        return pltpu.make_async_remote_copy(
            src_ref=zb.at[src, pair], dst_ref=zb.at[dst, pair],
            send_sem=zsend.at[dst, pair], recv_sem=zrecv.at[dst, pair],
            device_id=zdev(1 if way == 0 else 7), device_id_type=MESH,
        )

    def d_copy(i):
        return pltpu.make_async_remote_copy(
            src_ref=zb.at[i], dst_ref=sb.at[i], send_sem=dsend.at[i], recv_sem=drecv.at[i],
            device_id=sib, device_id_type=MESH,
        )

    def hand_over(places, far):
        @pl.when(match if far % 2 else jnp.logical_not(match))
        def _():
            for i in places:
                d_copy(i).start()

    def t_copy(pair):
        rows = pl.ds(pl.multiple_of((1 - k) * (LEN // 2), 32), LEN // 2)
        return pltpu.make_async_remote_copy(
            src_ref=tb.at[rows], dst_ref=zb.at[7, pair], send_sem=tsend.at[0],
            recv_sem=trecv.at[0], device_id=sib, device_id_type=MESH,
        )

    def z_turn():
        for b in range(2):
            pltpu.make_async_copy(xp, lb.at[b], lrecv.at[b]).wait()
        parts = [lb[b, :, i * LEN : (i + 1) * LEN] for b in range(2) for i in range(2)]
        tb[...] = dot(eye, jnp.concatenate(parts, axis=0), NT).astype(BF16)
        t_copy(k).start()
        zb[7, k] = tb[pl.ds(pl.multiple_of(k * (LEN // 2), 32), LEN // 2)]

    def z_begin(pair):
        @pl.when(pair == k)
        def _():
            z_turn()

        @pl.when(pair != k)
        def _():
            t_copy(1 - k).wait_recv()

        for way in range(2):
            z_copy(7, way, pair, way).start()

    def relay(far, pair):
        for way in range(2):
            place = 2 * (far - 1) + way
            z_copy(place, place, pair, way).wait_recv()
            if far < 3:
                z_copy(place, place + 2, pair, way).start()
            else:
                @pl.when(pair == way)
                def _():
                    z_copy(place, 6, pair, way).start()

    def finish_z():
        for way in range(2):
            z_copy(6, 6, way, way).wait_recv()
        hand_over((6,), 4)

    def ahead(f, *args):
        pl.when(yh == yl)(lambda: f(*args))

    def behind(f, *args):
        pl.when(yh != yl)(lambda: f(*args))

    def begin_later():
        z_begin(later)
        hand_over((7,), 0)

    def relay_later(far):
        relay(far, later)
        hand_over((2 * far - 2, 2 * far - 1), far)

    ahead(z_begin, soon)
    dkv[...] = jnp.zeros_like(dkv)
    dqt[...] = jnp.zeros_like(dqt)
    ks.wait_recv()
    kt[0] = dot(eye_wide, kb[0:PAIR], NT).astype(BF16)
    q1.wait_recv()
    q3 = go(remote(slot(qb, 1), slot(qb, 3), xdev(1)))
    g2.wait_recv()
    g3 = go(remote(slot(gb, 2), slot(gb, 3), xdev(3)))

    def attend(m, t):
        keys_at = slice(m * PAIR, (m + 1) * PAIR)
        tile = pl.ds(pl.multiple_of(t * TILE, TILE), TILE)
        qs, grads, stats = qb[tile], gb[tile], stp[t]
        keys = kb[keys_at]
        up = dot(vb[keys_at], grads, NT)
        score1 = dot(keys[:, :HALF], qs[:, :HALF], NT)
        score2 = dot(keys[:, HALF:], qs[:, HALF:], NT)
        s1, s2, mix = [], [], []
        for b in range(2):
            part = slice(b * LEN, (b + 1) * LEN)
            key_pos = position((yl + m) % 2, x, (k + b) % 2)
            hide = jnp.where(stats[4:5] < key_pos, 1e30, 0.0)
            p1 = jnp.exp2(score1[part] * (SCALE * LOG2E) - (stats[0:1] + hide))
            p2 = jnp.exp2(score2[part] * (SCALE * LOG2E) - (stats[1:2] + hide))
            if m == 0 and b == 0:
                key_row = lax.broadcasted_iota(jnp.int32, (LEN, TILE), 0)
                query_col = lax.broadcasted_iota(jnp.int32, (LEN, TILE), 1) + t * TILE
                p1 = jnp.where(key_row <= query_col, p1, 0.0)
                p2 = jnp.where(key_row <= query_col, p2, 0.0)
            s1.append((p1 * (up[part] - stats[2:3])).astype(BF16))
            s2.append((p2 * (up[part] - stats[3:4])).astype(BF16))
            mix.append((p1 - p2).astype(BF16))
        s1, s2, mix = (jnp.concatenate(a, axis=0) for a in (s1, s2, mix))
        dkv[keys_at, 0:HALF] += dot(s1, qs[:, :HALF])
        dkv[keys_at, HALF:WIDE] += dot(s2, qs[:, HALF:])
        dkv[keys_at, WIDE:] += dot(mix, grads)
        dqt[t, 0:HALF] += dot(kt[m, 0:HALF, :], s1)
        dqt[t, HALF:WIDE] += dot(kt[m, HALF:WIDE, :], s2)

    def sweep(m, low, high):
        def step(t, carry):
            attend(m, t)
            return carry

        lax.fori_loop(low, high, step, 0)

    def signed(t):
        sign = jnp.where(lax.broadcasted_iota(jnp.int32, (1, WIDE), 1) < HALF, SCALE, -SCALE)
        return t * sign

    def both_cores(j, i):
        sib_s[i] = dkv[j * LEN : (j + 1) * LEN].astype(BF16)
        return go(remote(sib_s.at[i], sib_r.at[i], sib))

    g1.wait_recv()
    gs[0].wait_recv()
    vs.wait_recv()
    behind(z_begin, soon)
    q2.wait_recv()
    gs[1].wait_recv()
    near = jnp.concatenate([st[0], st[1], st[2]], axis=1)
    for t in range(3):
        stp[t] = near[:, t * TILE : (t + 1) * TILE]
    sweep(0, 0, 2)
    ahead(relay, 1, soon)
    sweep(0, 2, 3)
    kp.wait_recv()
    rk = go(remote(slot(kb, 2), slot(kb, 3), sib))
    vp.wait_recv()
    rv = go(remote(slot(vb, 2), slot(vb, 3), sib))
    ahead(begin_later)
    behind(relay, 1, soon)
    rk.wait_recv()
    rv.wait_recv()
    kt[1] = dot(eye_wide, kb[PAIR:ALL], NT).astype(BF16)
    sweep(1, 0, 3)

    def turn_dq(t):
        dqf[t * TILE : (t + 1) * TILE] = dqt[t].T

    def send_dq(s, d):
        dqs[s - 1] = dqf[s * LEN : (s + 1) * LEN].astype(BF16)
        return go(remote(dqs.at[s - 1], dqr.at[s - 1], xdev(d)))

    for t in range(3):
        turn_dq(t)
    sq = [send_dq(1, 3)]
    ahead(relay, 2, soon)
    behind(begin_later)

    q3.wait_recv()
    g3.wait_recv()
    gs[2].wait_recv()
    far = jnp.concatenate([st[2], st[3]], axis=1)
    for t in (3, 4):
        stp[t] = far[:, t * TILE - 2 * LEN : (t + 1) * TILE - 2 * LEN]
    sweep(1, 3, 5)
    b0 = both_cores(3, 0)
    sweep(0, 3, 5)
    ahead(relay_later, 1)
    b1 = both_cores(1, 1)
    turn_dq(3)
    turn_dq(4)
    sq.append(send_dq(3, 2))
    sq.append(send_dq(2, 1))

    def rows_of(yl_, k_):
        return pl.ds(pl.multiple_of((yl_ * 2 + k_) * LEN, LEN), LEN)

    columns = (None, slice(0, WIDE), slice(WIDE, 2 * WIDE))

    def chip_sum(i, b):
        return dkv[2 * b * LEN : (2 * b + 1) * LEN, columns[i]] + sib_r[1 - b, :, columns[i]].astype(F32)

    def exchange(i, b):
        par_s[b, i - 1] = chip_sum(i, b).astype(BF16)
        return go(remote(par_s.at[b, i - 1], par_r.at[1 - b, i - 1], par))

    def total(i, b, came):
        came.wait_recv()
        value = chip_sum(i, b) + par_r[b, i - 1].astype(F32)
        value = (signed(value) if i == 1 else value).astype(BF16)
        ref = gw.at[i, rows_of(yl if b == 0 else 1 - yl, k)]
        ref[...] = value
        if b == 0:
            (dk_out if i == 1 else dv_out)[...] = value
        return go(remote(ref, ref, sib))

    b0.wait_recv()
    e1 = exchange(1, 1)
    b1.wait_recv()
    e0 = exchange(1, 0)
    behind(relay, 2, soon)
    f1 = exchange(2, 1)
    ahead(relay, 3, soon)
    c_own = total(1, 0, e1)
    behind(relay_later, 1)
    for cp in sq:
        cp.wait_recv()
    value = dqf[0:LEN]
    for i in range(3):
        value = value + dqr[i].astype(F32)
    value = signed(value).astype(BF16)
    dq_out[...] = value
    ref = gw.at[0, rows_of(yl, k)]
    ref[...] = value
    q_par = go(remote(ref, ref, par))
    q_sib = go(remote(ref, ref, sib))
    ahead(relay_later, 2)
    c_par = total(1, 1, e0)
    f0 = exchange(2, 0)
    behind(relay, 3, soon)

    def h_copy(i, way):
        return pltpu.make_async_remote_copy(
            src_ref=ws.at[2, i, pl.ds(way * (LEN // 2), LEN // 2)], dst_ref=hr.at[way, i],
            send_sem=hsend.at[way, i], recv_sem=hrecv.at[way, i],
            device_id=xdev(1 if way == 0 else 3), device_id_type=MESH,
        )

    def w_copy(i, way):
        return pltpu.make_async_remote_copy(
            src_ref=ws.at[way, i], dst_ref=wr.at[way, i],
            send_sem=wsend.at[way, i], recv_sem=wrecv.at[way, i],
            device_id=xdev(1 if way == 0 else 3), device_id_type=MESH,
        )

    def place_of(r):
        ahead = (2 * ((x + r) % 4) + k - z + 8) % 8
        place = jnp.where(ahead == 0, 7, 6)
        for far, at in ((1, 1), (7, 0), (2, 3), (6, 2), (3, 5), (5, 4)):
            place = jnp.where(ahead == far, at, place)
        return place

    own_half = pl.ds(pl.multiple_of(k * (LEN // 2), 32), LEN // 2)
    other_half = pl.ds(pl.multiple_of((1 - k) * (LEN // 2), 32), LEN // 2)

    def project(i, r):
        p = place_of(r)
        chunk = [jnp.concatenate([ref[p, 0], ref[p, 1]], axis=1) for ref in (zb, sb)]
        part = dot(jnp.concatenate(chunk, axis=0), gw[i])
        if r == 2:
            ws[2, i, own_half] = part[: LEN // 2].astype(BF16)
            ws[2, i, other_half] = part[LEN // 2 :].astype(BF16)
            for way in range(2):
                h_copy(i, way).start()
        else:
            to = w_out.at[i] if r == 0 else pp.at[r // 2, i]
            to[own_half] = part[: LEN // 2]
            to[other_half] = part[LEN // 2 :]

    def forward(i):
        for way in range(2):
            rows = slice(way * (LEN // 2), (way + 1) * (LEN // 2))
            rest = slice((1 - way) * (LEN // 2), (2 - way) * (LEN // 2))
            ws[way, i, rest] = pp[way, i, rest].astype(BF16)
            h_copy(i, way).wait_recv()
            ws[way, i, rows] = (pp[way, i, rows] + hr[way, i].astype(F32)).astype(BF16)
            w_copy(i, way).start()

    c_own.wait_recv()
    c_par.wait_recv()
    q_par.wait_recv()
    ref = gw.at[0, rows_of(1 - yl, k)]
    q_far = go(remote(ref, ref, sib))
    ahead(relay_later, 3)
    behind(relay_later, 2)
    q_sib.wait_recv()
    q_far.wait_recv()
    c_own = total(2, 0, f1)
    ahead(finish_z)
    c_par = total(2, 1, f0)
    behind(relay_later, 3)
    behind(finish_z)
    for r in range(4):
        d_copy(place_of(r)).wait_recv()
    for r in (2, 1, 3):
        project(1, r)
    project(0, 2)
    forward(1)
    project(0, 1)
    project(0, 3)
    project(1, 0)
    c_own.wait_recv()
    c_par.wait_recv()
    project(2, 2)
    forward(0)
    project(2, 1)
    project(2, 3)
    project(0, 0)
    forward(2)
    project(2, 0)
    for i in (1, 0, 2):
        for way in range(2):
            w_copy(i, way).wait_recv()
        w_out[i] += wr[0, i].astype(F32) + wr[1, i].astype(F32)

    for cp in pending:
        cp.wait_send()

    @pl.when(jnp.logical_not(mine))
    def _():
        l_copy(0).wait_send()

    l_copy(1).wait_send()
    t_copy(k).wait_send()
    for place in range(6):
        for pair in range(2):
            z_copy(7, place, pair, 0).wait_send()
    for pair in range(2):
        z_copy(7, 6, pair, pair).wait_send()
    for far, places in ((0, (7,)), (1, (0, 1)), (2, (2, 3)), (3, (4, 5)), (4, (6,))):
        @pl.when(match if far % 2 else jnp.logical_not(match))
        def _():
            for i in places:
                d_copy(i).wait_send()

    for i in range(3):
        for way in range(2):
            h_copy(i, way).wait_send()
            w_copy(i, way).wait_send()


def tail(a, b, c, d, a_out, b_out, c_out, d_out, sems):
    copies = [
        pltpu.make_async_copy(src, dst, sems.at[i])
        for i, (src, dst) in enumerate(((d, d_out), (a, a_out), (b, b_out), (c, c_out)))
    ]
    for cp in copies:
        cp.start()
    for cp in copies:
        cp.wait()


def body(*args):
    vmem = pl.BlockSpec(memory_space=pltpu.VMEM)
    smem = pl.BlockSpec(memory_space=pltpu.SMEM)
    grad = jax.ShapeDtypeStruct((LEN, WIDE), BF16)
    dma = pltpu.SemaphoreType.DMA
    shapes = (grad, grad, grad, jax.ShapeDtypeStruct((3, LEN, WIDE), F32))
    results = pl.pallas_call(
        kernel,
        out_shape=shapes,
        in_specs=[vmem] * 8 + [smem] * 2,
        out_specs=(vmem,) * 4,
        scratch_shapes=[
            pltpu.VMEM((ALL, WIDE), BF16),
            pltpu.VMEM((ALL, WIDE), BF16),
            pltpu.VMEM((4, 8, LEN), F32),
            pltpu.VMEM((5, 8, TILE), F32),
            pltpu.VMEM((ALL, WIDE), BF16),
            pltpu.VMEM((ALL, WIDE), BF16),
            pltpu.VMEM((2, WIDE, PAIR), BF16),
            pltpu.VMEM((ALL, 2 * WIDE), F32),
            pltpu.VMEM((5, WIDE, TILE), F32),
            pltpu.VMEM((ALL, WIDE), F32),
            pltpu.VMEM((3, LEN, WIDE), BF16),
            pltpu.VMEM((3, LEN, WIDE), BF16),
            pltpu.VMEM((2, LEN, 2 * WIDE), BF16),
            pltpu.VMEM((2, LEN, 2 * WIDE), BF16),
            pltpu.VMEM((2, 2, LEN, WIDE), BF16),
            pltpu.VMEM((2, 2, LEN, WIDE), BF16),
            pltpu.VMEM((3, ALL, WIDE), BF16),
            pltpu.VMEM((LEN // 2, PAIR), BF16),
            pltpu.VMEM((2, LEN // 2, PAIR), BF16),
            pltpu.VMEM((LEN, PAIR), BF16),
            pltpu.VMEM((8, 2, LEN // 2, PAIR), BF16),
            pltpu.VMEM((8, 2, LEN // 2, PAIR), BF16),
            pltpu.VMEM((2, 3, LEN, WIDE), F32),
            pltpu.VMEM((2, 3, LEN // 2, WIDE), BF16),
            pltpu.VMEM((3, 3, LEN, WIDE), BF16),
            pltpu.VMEM((2, 3, LEN, WIDE), BF16),
            dma((32,)),
            dma((32,)),
            dma((7, 2)),
            dma((7, 2)),
            dma((8,)),
            dma((8,)),
            dma((1,)),
            dma((1,)),
            dma((2,)),
            dma((2,)),
            dma((2, 3)),
            dma((2, 3)),
            dma((2, 3)),
            dma((2, 3)),
        ],
        compiler_params=pltpu.CompilerParams(
            collective_id=0, has_side_effects=True, vmem_limit_bytes=56 * 2**20
        ),
        name="diff_attention_backward",
    )(*args)
    return pl.pallas_call(
        tail,
        out_shape=shapes,
        in_specs=[vmem] * 4,
        out_specs=(pl.BlockSpec(memory_space=pl.ANY),) * 4,
        scratch_shapes=[dma((4,))],
        name="write_results",
    )(*results)


def solution(mesh):
    in_specs = (P("ctx", "head"),) * 7 + (P(None, "head", "ctx"), P("head"), P())
    out_specs = (P("ctx", "head"), P("ctx", "head"), P("ctx", "head"), P(None, "ctx", "head"))
    return jax.shard_map(body, mesh=mesh, in_specs=in_specs, out_specs=out_specs, check_vma=False)
```

time: 92.4 us -> 87.3 us (0.945); the launches traced: 91.2 us -> 87.2 us
  local copies, waits for them, and re-layouts: 5.81 us -> 0 us
  Pallas kernels: 84.1 us -> 85.9 us
    unnamed x6 -> x0, local copies, waits for them, and re-layouts: 5.81 us -> none
    pallas_call x1 -> x2, Pallas kernels: 84.1 us -> 85.9 us  [the longest x1 83.3 us: body(): pl.pallas_call(kernel, out_shape=shapes, in_specs=[vmem] * 8 + [smem] * 2...]
where the time goes in v2:
time: 87.3 us; the launch traced here: 87.2 us
  Pallas kernels  85.9 us (98%)
  between operations  1.29 us (1%)
    pallas_call x1, Pallas kernels, body(): pl.pallas_call(kernel, out_shape=shapes, in_specs=[vmem] * 8 + [smem] * 2...  83.3 us
    pallas_call x1, Pallas kernels, body(): pl.pallas_call(tail, out_shape=shapes, in_specs=[vmem] * 4, out_specs=(pl...  2.59 us

profile of v2, /device:TPU:8, one launch (start us, length us, event | category | flops | bytes accessed | tf_op | source)
XLA Modules:
  0.0 87.2 jit_solution(10118130515614362706)
XLA Ops:
  1.3 83.3 %diff_attention_backward.1 = (bf16[320,256]{1,0:T(8,128)(2,1)}, bf16[320,256]{1,0:T(8,128)(2,1)}, bf16[320,256]{1,0:T(8,128)(2,1)}, f32[3,320,256]{2,1,0:T(8,128)}) custom-call(bf16[320,320]{1,0:T(8,128)(2,1)} %x_ref.1, bf16[320,256]{1,0:T(8,128)(2,1)} %q_ref.1, bf16[320,256]{1,0:T(8,128)(2,1)} %k_ref.1, bf16[320,256]{1,0:T(8,128)(2,1)} %v_ref.1, ...), custom_call_target="tpu_custom_call" | custom-call | tf_op jit(solution)/shard_map/diff_attention_backward/pallas_call | solution.py:508
  84.6 2.6 %write_results.1 = (bf16[320,256]{1,0:T(8,128)(2,1)}, bf16[320,256]{1,0:T(8,128)(2,1)}, bf16[320,256]{1,0:T(8,128)(2,1)}, f32[3,320,256]{2,1,0:T(8,128)}) custom-call(bf16[320,256]{1,0:T(8,128)(2,1)} %get-tuple-element.8.a, bf16[320,256]{1,0:T(8,128)(2,1)} %get-tuple-element.9.b, bf16[320,256]{1,0:T(8,128)(2,1)} %get-tuple-element.10.c, ...), custom_call_target="tpu_custom_call" | custom-call | tf_op jit(solution)/shard_map/write_results/pallas_call | solution.py:560

commit v3 on v2

--- a/solution.py
+++ b/solution.py
@@ -97,7 +97,9 @@
     def _():
         l_local.start()
 
-    l_copy(1).start()
+    @pl.when(yh != yl)
+    def _():
+        l_copy(1).start()
 
     @pl.when(jnp.logical_not(mine))
     def _():
@@ -231,6 +233,11 @@
     kt[0] = dot(eye_wide, kb[0:PAIR], NT).astype(BF16)
     q1.wait_recv()
     q3 = go(remote(slot(qb, 1), slot(qb, 3), xdev(1)))
+
+    @pl.when(yh == yl)
+    def _():
+        l_copy(1).start()
+
     g2.wait_recv()
     g3 = go(remote(slot(gb, 2), slot(gb, 3), xdev(3)))
 
@@ -434,15 +441,19 @@
     behind(relay_later, 2)
     q_sib.wait_recv()
     q_far.wait_recv()
+
+    def first_sums():
+        finish_z()
+        for r in range(4):
+            d_copy(place_of(r)).wait_recv()
+        for r in (2, 1, 3):
+            project(1, r)
+
+    ahead(first_sums)
     c_own = total(2, 0, f1)
-    ahead(finish_z)
     c_par = total(2, 1, f0)
     behind(relay_later, 3)
-    behind(finish_z)
-    for r in range(4):
-        d_copy(place_of(r)).wait_recv()
-    for r in (2, 1, 3):
-        project(1, r)
+    behind(first_sums)
     project(0, 2)
     forward(1)
     project(0, 1)

time: 87.3 us -> 86.2 us (0.987)
  Pallas kernels: 85.9 us -> 84.8 us
    pallas_call x1, Pallas kernels: 83.3 us -> 82.2 us  [body(): pl.pallas_call(kernel, out_shape=shapes, in_specs=[vmem] * 8 + [smem] * 2...]
where the time goes in v3:
time: 86.2 us; the launch traced here: 86.1 us
  Pallas kernels  84.8 us (98%)
  between operations  1.29 us (1%)
    pallas_call x1, Pallas kernels, body(): pl.pallas_call(kernel, out_shape=shapes, in_specs=[vmem] * 8 + [smem] * 2...  82.2 us
    pallas_call x1, Pallas kernels, body(): pl.pallas_call(tail, out_shape=shapes, in_specs=[vmem] * 4, out_specs=(pl...  2.59 us

profile of v3, /device:TPU:8, one launch (start us, length us, event | category | flops | bytes accessed | tf_op | source)
XLA Modules:
  0.0 86.1 jit_solution(11576250605367748096)
XLA Ops:
  1.3 82.2 %diff_attention_backward.1 = (bf16[320,256]{1,0:T(8,128)(2,1)}, bf16[320,256]{1,0:T(8,128)(2,1)}, bf16[320,256]{1,0:T(8,128)(2,1)}, f32[3,320,256]{2,1,0:T(8,128)}) custom-call(bf16[320,320]{1,0:T(8,128)(2,1)} %x_ref.1, bf16[320,256]{1,0:T(8,128)(2,1)} %q_ref.1, bf16[320,256]{1,0:T(8,128)(2,1)} %k_ref.1, bf16[320,256]{1,0:T(8,128)(2,1)} %v_ref.1, ...), custom_call_target="tpu_custom_call" | custom-call | tf_op jit(solution)/shard_map/diff_attention_backward/pallas_call | solution.py:519
  83.5 2.6 %write_results.1 = (bf16[320,256]{1,0:T(8,128)(2,1)}, bf16[320,256]{1,0:T(8,128)(2,1)}, bf16[320,256]{1,0:T(8,128)(2,1)}, f32[3,320,256]{2,1,0:T(8,128)}) custom-call(bf16[320,256]{1,0:T(8,128)(2,1)} %get-tuple-element.8.a, bf16[320,256]{1,0:T(8,128)(2,1)} %get-tuple-element.9.b, bf16[320,256]{1,0:T(8,128)(2,1)} %get-tuple-element.10.c, ...), custom_call_target="tpu_custom_call" | custom-call | tf_op jit(solution)/shard_map/write_results/pallas_call | solution.py:571

commit v4 on v3

--- a/solution.py
+++ b/solution.py
@@ -499,15 +499,9 @@
             w_copy(i, way).wait_send()
 
 
-def tail(a, b, c, d, a_out, b_out, c_out, d_out, sems):
-    copies = [
-        pltpu.make_async_copy(src, dst, sems.at[i])
-        for i, (src, dst) in enumerate(((d, d_out), (a, a_out), (b, b_out), (c, c_out)))
-    ]
-    for cp in copies:
-        cp.start()
-    for cp in copies:
-        cp.wait()
+def tail(a, b, c, d, a_out, b_out, c_out, d_out):
+    for src, dst in ((a, a_out), (b, b_out), (c, c_out), (d, d_out)):
+        dst[...] = src[...]
 
 
 def body(*args):
@@ -568,12 +562,15 @@
         ),
         name="diff_attention_backward",
     )(*args)
+    specs = [pl.BlockSpec((LEN // 2, WIDE), lambda i: (i, 0))] * 3
+    specs.append(pl.BlockSpec((3, LEN // 2, WIDE), lambda i: (0, i, 0)))
     return pl.pallas_call(
         tail,
         out_shape=shapes,
-        in_specs=[vmem] * 4,
-        out_specs=(pl.BlockSpec(memory_space=pl.ANY),) * 4,
-        scratch_shapes=[dma((4,))],
+        grid=(2,),
+        in_specs=specs,
+        out_specs=tuple(specs),
+        compiler_params=pltpu.CompilerParams(vmem_limit_bytes=56 * 2**20),
         name="write_results",
     )(*results)
 

time: 86.2 us -> 85.9 us (level)
  no operation moved by 1% of the time
where the time goes in v4:
time: 85.9 us; the launch traced here: 85.8 us
  Pallas kernels  84.5 us (98%)
  between operations  1.29 us (2%)
    pallas_call x1, Pallas kernels, body(): pl.pallas_call(kernel, out_shape=shapes, in_specs=[vmem] * 8 + [smem] * 2...  82.2 us
    pallas_call x1, Pallas kernels, body(): pl.pallas_call(tail, out_shape=shapes, grid=(2,), in_specs=specs, out_spe...  2.31 us

profile of v4, /device:TPU:8, one launch (start us, length us, event | category | flops | bytes accessed | tf_op | source)
XLA Modules:
  0.0 85.8 jit_solution(15557866929054118412)
XLA Ops:
  1.3 82.2 %diff_attention_backward.1 = (bf16[320,256]{1,0:T(8,128)(2,1)}, bf16[320,256]{1,0:T(8,128)(2,1)}, bf16[320,256]{1,0:T(8,128)(2,1)}, f32[3,320,256]{2,1,0:T(8,128)}) custom-call(bf16[320,320]{1,0:T(8,128)(2,1)} %x_ref.1, bf16[320,256]{1,0:T(8,128)(2,1)} %q_ref.1, bf16[320,256]{1,0:T(8,128)(2,1)} %k_ref.1, bf16[320,256]{1,0:T(8,128)(2,1)} %v_ref.1, ...), custom_call_target="tpu_custom_call" | custom-call | tf_op jit(solution)/shard_map/diff_attention_backward/pallas_call | solution.py:513
  83.5 2.3 %write_results.1 = (bf16[320,256]{1,0:T(8,128)(2,1)}, bf16[320,256]{1,0:T(8,128)(2,1)}, bf16[320,256]{1,0:T(8,128)(2,1)}, f32[3,320,256]{2,1,0:T(8,128)}) custom-call(bf16[320,256]{1,0:T(8,128)(2,1)} %get-tuple-element.8.a, bf16[320,256]{1,0:T(8,128)(2,1)} %get-tuple-element.9.b, bf16[320,256]{1,0:T(8,128)(2,1)} %get-tuple-element.10.c, ...), custom_call_target="tpu_custom_call" | custom-call | tf_op jit(solution)/shard_map/write_results/pallas_call | solution.py:567
